TPU v7x, 32 devices: a whole 2x2x4 slice. The times are simulated.
32 devices in a mesh: gx: 8 (over z, x), gy: 4 (over y, core).
Axes of the slice: x: 2, y: 2, z: 4, core: 2. Of those that a mesh axis runs over, the one named last changes fastest.
Arguments:
- e_field: float32 [3, 128, 128, 128], P(None, 'gx', 'gy'), may hold values from -6 to 6
- h_field: float32 [3, 128, 128, 128], P(None, 'gx', 'gy'), may hold values from -6 to 6
- lorentz_current: float32 [3, 128, 128, 128], P(None, 'gx', 'gy'), may hold values from -3 to 3
- polarization: float32 [3, 128, 128, 128], P(None, 'gx', 'gy'), may hold values from -3 to 3
- material_ids: int32 [128, 128, 128], P('gx', 'gy'), may hold values from 0 to 7
- inv_permittivity: float32 [8], replicated, may hold values from 0.3 to 1
- current_decay: float32 [8], replicated, may hold values from 0.4 to 0.95
- current_drive: float32 [8], replicated, may hold values from 0.3 to 1
- current_restore: float32 [8], replicated, may hold values from 0.2 to 1
- incident_line: float32 [2, 512], P(None, 'gy'), may hold values from -6 to 6
- boundary_mask: int32 [8, 4], replicated, may hold values 0 or 1
- surface_slots: int32 [8, 4, 128], P('gx', 'gy'), may hold values from -1 to 511, as said below
- block_owner: int32 [64], replicated, may hold values from 0 to 31, as said below
Outputs:
- e_out: float32 [3, 128, 128, 128], P(None, 'gx', 'gy')
- h_out: float32 [3, 128, 128, 128], P(None, 'gx', 'gy')
- j_out: float32 [3, 128, 128, 128], P(None, 'gx', 'gy')
- p_out: float32 [3, 128, 128, 128], P(None, 'gx', 'gy')
- far_field: float32 [128, 512], P(('gx', 'gy'))
Inputs may be any that keep to these rules, and one draw needn't show every extreme that they name: `block_owner`: each device number names at most 4 blocks, and some device names exactly 4. `surface_slots`: each tile lists distinct surface cells (x within the tile times 32 plus y within the tile) in its first slots and -1 in the rest; at least 32 slots are used on every tile, and some tile uses all 128.
All inputs are finite; a program needn't handle non-finite values.
Results may differ from a plain program's by a relative error of at most 0.0003.
Values sent between devices are 32-bit elements; how exact they have to be, the bound alone decides.
A program may use at most 64 MiB of HBM per device.

v0:
```python
import math

import jax
import jax.numpy as jnp
from jax import lax
from jax.sharding import PartitionSpec as P

STEPS = 4
NF = 2
DB = 32
BMAX = 4


FREQS = (0.35, 0.6)
WAVENUMS = (0.7, 1.2)
COURANT = 0.5
HIGHEST = lax.Precision.HIGHEST


def extended(x, sides, width):
    for axis, dim in sides:
        devices, length = (lax.axis_size(axis), x.shape[dim])
        up = [(i, (i + 1) % devices) for i in range(devices - 1)]
        down = [(j, i) for i, j in up]
        last = lax.slice_in_dim(x, length - width, length, axis=dim)
        leading = lax.slice_in_dim(x, 0, width, axis=dim)
        before = lax.ppermute(last, axis, up)
        after = lax.ppermute(leading, axis, down)
        x = jnp.concatenate([before, x, after], axis=dim)
    return x


def forward_diff(values, which_axis):
    length = values.shape[which_axis]
    upper_part = lax.slice_in_dim(values, 1, length, axis=which_axis)
    widths = [(0, 0)] * values.ndim
    widths[which_axis] = (0, 1)
    return jnp.pad(upper_part, widths) - values


def backward_diff(values, which_axis):
    length = values.shape[which_axis]
    lower_part = lax.slice_in_dim(values, 0, length - 1, axis=which_axis)
    widths = [(0, 0)] * values.ndim
    widths[which_axis] = (1, 0)
    return values - jnp.pad(lower_part, widths)


def advance_magnetic(e_line, h_line):
    e_ahead = jnp.concatenate([e_line[1:], jnp.zeros((1,), e_line.dtype)])
    return h_line - COURANT * (e_ahead - e_line)


def advance_electric(e_line, h_line):
    h_behind = jnp.concatenate([jnp.zeros((1,), h_line.dtype), h_line[:-1]])
    return e_line - COURANT * (h_line - h_behind)


def directions(dir_index, total_dirs):
    along_u = ((dir_index % 64).astype(jnp.float32) + 0.5) / 32.0 - 1.0
    along_v = ((dir_index // 64).astype(jnp.float32) + 0.5) * (128.0 / total_dirs) - 1.0
    return (along_u, along_v)


def radiate(slot_rows, coords_x, coords_y, along_u, along_v):
    spread = along_u[:, None] * coords_x[None, :] + along_v[:, None] * coords_y[None, :]
    pieces_out = []
    for freq_index in range(len(WAVENUMS)):
        phases = WAVENUMS[freq_index] * spread
        cosine = jnp.cos(phases)
        sine_part = jnp.sin(phases)
        real_rows = slot_rows[freq_index * 8 : freq_index * 8 + 8 : 2]
        imag_rows = slot_rows[freq_index * 8 + 1 : freq_index * 8 + 8 : 2]
        real_out = jnp.dot(real_rows, cosine.T, precision=HIGHEST) - jnp.dot(
            imag_rows, sine_part.T, precision=HIGHEST
        )
        imag_out = jnp.dot(imag_rows, cosine.T, precision=HIGHEST) + jnp.dot(
            real_rows, sine_part.T, precision=HIGHEST
        )
        pieces_out.append(jnp.stack([real_out, imag_out], axis=1).reshape(8, -1))
    return jnp.concatenate(pieces_out, axis=0)


def slot_table(block_owner, per_device):
    count_blocks = block_owner.shape[0]
    order_ids = jnp.arange(count_blocks, dtype=jnp.int32)
    earlier = (order_ids[None, :] < order_ids[:, None]) & (
        block_owner[None, :] == block_owner[:, None]
    )
    rank_in = jnp.sum(earlier.astype(jnp.int32), axis=1)
    return block_owner * per_device + rank_in


def lookup(coef_table, material_ids):
    kind_ids = jnp.arange(coef_table.shape[0], dtype=jnp.int32)
    matches = material_ids[None] == kind_ids[:, None, None, None]
    return jnp.sum(jnp.where(matches, coef_table[:, None, None, None], 0.0), axis=0)


def shards(
    e_field,
    h_field,
    lorentz_current,
    polarization,
    material_ids,
    inv_permittivity,
    current_decay,
    current_drive,
    current_restore,
    incident_line,
    boundary_mask,
    surface_slots,
    block_owner,
):
    cells_x = e_field.shape[1]
    cells_y = e_field.shape[2]
    depth_cells = e_field.shape[3]
    tiles_y = lax.axis_size("gy")
    tile_count = lax.axis_size("gx") * tiles_y
    index_x = lax.axis_index("gx")
    index_y = lax.axis_index("gy")
    inv_eps = lookup(inv_permittivity, material_ids)
    decay_cell = lookup(current_decay, material_ids)
    drive_cell = lookup(current_drive, material_ids)
    restore_cell = lookup(current_restore, material_ids)
    whole_line = lax.all_gather(incident_line, "gy", axis=1, tiled=True)
    e_line = whole_line[0]
    h_line = whole_line[1]
    line_length = e_line.shape[0]
    plane_lower = depth_cells // 4
    plane_surface = plane_lower - 3
    region_x = jnp.arange(cells_x + 1, dtype=jnp.int32)
    region_y = jnp.arange(cells_y + 1, dtype=jnp.int32)
    global_x = index_x * cells_x + region_x - 1
    global_y = index_y * cells_y + region_y - 1
    inject_index = jnp.clip(2 * (global_x[:, None] + global_y[None, :]) + 1, 0, line_length - 1)
    own_flag = lax.dynamic_slice(boundary_mask, (index_x, index_y), (1, 1))[0, 0]
    left_flag = lax.dynamic_slice(boundary_mask, (jnp.maximum(index_x - 1, 0), index_y), (1, 1))[
        0, 0
    ]
    below_flag = lax.dynamic_slice(boundary_mask, (index_x, jnp.maximum(index_y - 1, 0)), (1, 1))[
        0, 0
    ]
    edge_x = region_x[:, None] == 0
    edge_y = region_y[None, :] == 0
    region_mask = jnp.where(edge_x, left_flag, jnp.where(edge_y, below_flag, own_flag)).astype(
        jnp.float32
    )
    ghost_keep = jnp.where(edge_x & (index_x == 0) | edge_y & (index_y == 0), 0.0, 1.0).astype(
        jnp.float32
    )
    depth_index = jnp.arange(depth_cells, dtype=jnp.int32)
    plane_h = depth_index == plane_lower - 1
    plane_e = depth_index == plane_lower
    e_now, h_now, j_now, p_now = (e_field, h_field, lorentz_current, polarization)
    currents = jnp.zeros((NF, 4, 2, cells_x, cells_y), jnp.float32)
    for step_index in range(STEPS):
        stacked = jnp.concatenate([e_now, h_now], axis=0)
        padded = extended(stacked, (("gx", 1), ("gy", 2)), 1)
        e_pad = padded[0:3]
        h_old = padded[3:6, : cells_x + 1, : cells_y + 1]
        e_base = e_pad[:, : cells_x + 1, : cells_y + 1]
        ahead_x = e_pad[:, 1:, : cells_y + 1] - e_base
        ahead_y = e_pad[:, : cells_x + 1, 1:] - e_base
        inject_e = e_line[inject_index] * region_mask
        h_x = h_old[0] - COURANT * (ahead_y[2] - forward_diff(e_base[1], 2))
        h_y = (
            h_old[1]
            - COURANT * (forward_diff(e_base[0], 2) - ahead_x[2])
            + COURANT * jnp.where(plane_h, inject_e[:, :, None], 0.0)
        )
        h_z = h_old[2] - COURANT * (ahead_x[1] - ahead_y[0])
        h_region = jnp.stack([h_x, h_y, h_z]) * ghost_keep[None, :, :, None]
        h_line = advance_magnetic(e_line, h_line)
        inject_h = h_line[inject_index[1:, 1:]] * region_mask[1:, 1:]
        h_own = h_region[:, 1:, 1:]
        behind_x = h_own - h_region[:, :-1, 1:]
        behind_y = h_own - h_region[:, 1:, :-1]
        curl_x = (
            behind_y[2] - backward_diff(h_own[1], 2) + jnp.where(plane_e, inject_h[:, :, None], 0.0)
        )
        curl_y = backward_diff(h_own[0], 2) - behind_x[2]
        curl_z = behind_x[1] - behind_y[0]
        curl_all = jnp.stack([curl_x, curl_y, curl_z])
        e_new = e_now + inv_eps[None] * (COURANT * curl_all - j_now)
        j_new = decay_cell[None] * j_now + drive_cell[None] * e_new - restore_cell[None] * p_now
        p_new = p_now + j_new
        e_line = advance_electric(e_line, h_line)
        tangential = jnp.stack(
            [
                e_new[0, :, :, plane_surface],
                e_new[1, :, :, plane_surface],
                h_own[0, :, :, plane_surface],
                h_own[1, :, :, plane_surface],
            ]
        )
        time_index = step_index + 1
        for freq_index in range(NF):
            weight_cos = math.cos(FREQS[freq_index] * time_index)
            weight_sin = math.sin(FREQS[freq_index] * time_index)
            currents = currents.at[freq_index, :, 0].add(weight_cos * tangential)
            currents = currents.at[freq_index, :, 1].add(-weight_sin * tangential)
        e_now = e_new
        h_now = h_own
        j_now = j_new
        p_now = p_new
    own_slots = surface_slots.reshape(-1)
    slot_count = own_slots.shape[0]
    slot_valid = (own_slots >= 0).astype(jnp.float32)
    slot_local = jnp.maximum(own_slots, 0)
    slot_rows = currents.reshape(8 * NF, cells_x * cells_y)[:, slot_local] * slot_valid[None, :]
    coords_x = (index_x * cells_x + slot_local // cells_y).astype(jnp.float32)
    coords_y = (index_y * cells_y + slot_local % cells_y).astype(jnp.float32)
    block_count = block_owner.shape[0]
    total_dirs = block_count * DB
    row_width = 8 * NF * DB
    far_scale = 1.0 / math.sqrt(tile_count * slot_count)
    slot_of = slot_table(block_owner, BMAX)
    dir_span = min(512, total_dirs)

    def one_block(first_dir):
        along_u, along_v = directions(first_dir + jnp.arange(dir_span, dtype=jnp.int32), total_dirs)
        return radiate(slot_rows, coords_x, coords_y, along_u, along_v)

    firsts = jnp.arange(total_dirs // dir_span, dtype=jnp.int32) * dir_span
    blocks = lax.map(one_block, firsts)
    spectrum = jnp.transpose(blocks, (1, 0, 2)).reshape(8 * NF, block_count, DB)
    spectrum = jnp.transpose(spectrum, (1, 0, 2)).reshape(block_count, row_width)
    onehot = (slot_of[None, :] == jnp.arange(tile_count * BMAX, dtype=jnp.int32)[:, None]).astype(
        jnp.float32
    )
    placed = jnp.dot(onehot, spectrum, precision=HIGHEST)
    received = lax.all_to_all(placed, ("gx", "gy"), split_axis=0, concat_axis=0, tiled=True)
    far_field = jnp.sum(received.reshape(tile_count, BMAX, row_width), axis=0) * far_scale
    return (e_now, h_now, j_now, p_now, far_field)


def solution(mesh):
    in_specs = (
        P(None, "gx", "gy", None),
        P(None, "gx", "gy", None),
        P(None, "gx", "gy", None),
        P(None, "gx", "gy", None),
        P("gx", "gy", None),
        P(),
        P(),
        P(),
        P(),
        P(None, "gy"),
        P(),
        P("gx", "gy", None),
        P(),
    )
    out_specs = (
        P(None, "gx", "gy", None),
        P(None, "gx", "gy", None),
        P(None, "gx", "gy", None),
        P(None, "gx", "gy", None),
        P(("gx", "gy"), None),
    )
    return jax.shard_map(shards, mesh=mesh, in_specs=in_specs, out_specs=out_specs, check_vma=False)
```

profile of v0, /device:TPU:0, one launch (start us, length us, event | category | flops | bytes accessed | tf_op | source)
XLA Modules:
  0.0 199.1 jit_solution(2570721244143975446)
XLA Ops:
  3.0 4.8 %collective-permute-start = (f32[6,1,32,128]{3,2,1,0:T(8,128)S(1)}, f32[6,1,32,128]{3,2,1,0:T(8,128)S(1)}, u32[]{:S(2)}, u32[]{:S(2)}) collective-permute-start(f32[6,1,32,128]{3,2,1,0:T(8,128)S(1)} %get-tuple-element.553), channel_id=1, source_target_pairs={{0,4},{4,8},{8,12},{12,16},{16,20},{20,24},{24,28},{1,5},{5,9},{9,... | collective-permute-start | bytes 294920 | tf_op jit(solution)/shard_map/ppermute | solution.py:27
  7.9 1.3 collective-permute-start.1
  9.2 5.1 %all_gather.3 = f32[2,512]{1,0:T(2,128)S(1)} all-gather(f32[2,128]{1,0:T(2,128)S(1)} %copy-done.7), channel_id=1, replica_groups=mesh['gx'=8,'gy'=4] {'gy'}, dimensions={1}, use_global_device_ids=true | all-gather | bytes 5120 | tf_op jit(solution)/shard_map/all_gather | solution.py:126
  15.0 4.0 %gather_fusion.4 = f32[561]{0:T(1024)S(1)} fusion(f32[512]{0:T(512)S(1)} %fusion.192, s32[1024]{0:T(1024)S(1)} %pad_clamp_fusion.2), kind=kCustom, calls=%fused_computation.4 | custom fusion | bytes 6732 | tf_op jit(solution)/shard_map/gather | solution.py:165
  19.0 4.0 %gather_fusion.2 = f32[561]{0:T(1024)S(1)} fusion(f32[512]{0:T(512)S(1)} %fusion.189, s32[1024]{0:T(1024)S(1)} %pad_clamp_fusion.2), kind=kCustom, calls=%fused_computation.2 | custom fusion | bytes 6732 | tf_op jit(solution)/shard_map/gather | solution.py:165
  23.0 4.0 %gather_fusion = f32[561]{0:T(1024)S(1)} fusion(f32[512]{0:T(512)S(1)} %bitcast.398, s32[1024]{0:T(1024)S(1)} %pad_clamp_fusion.2), kind=kCustom, calls=%fused_computation | custom fusion | bytes 6732 | tf_op jit(solution)/shard_map/gather | solution.py:165
  27.1 4.0 %gather_fusion.6 = f32[561]{0:T(1024)S(1)} fusion(f32[512]{0:T(512)S(1)} %fusion.195, s32[1024]{0:T(1024)S(1)} %pad_clamp_fusion.2), kind=kCustom, calls=%fused_computation.6 | custom fusion | bytes 6732 | tf_op jit(solution)/shard_map/gather | solution.py:165
  31.5 3.5 %gather_fusion.5 = f32[512]{0:T(512)S(1)} fusion(f32[512]{0:T(512)S(1)} %fusion.204, s32[1024]{0:T(1024)S(1)} %get-tuple-element.596), kind=kCustom, calls=%fused_computation.5 | custom fusion | bytes 6144 | tf_op jit(solution)/shard_map/gather | solution.py:175
  35.0 3.5 %gather_fusion.3 = f32[512]{0:T(512)S(1)} fusion(f32[512]{0:T(512)S(1)} %fusion.201, s32[1024]{0:T(1024)S(1)} %get-tuple-element.596), kind=kCustom, calls=%fused_computation.3 | custom fusion | bytes 6144 | tf_op jit(solution)/shard_map/gather | solution.py:175
  38.5 3.5 %gather_fusion.1 = f32[512]{0:T(512)S(1)} fusion(f32[512]{0:T(512)S(1)} %fusion.198, s32[1024]{0:T(1024)S(1)} %get-tuple-element.596), kind=kCustom, calls=%fused_computation.1 | custom fusion | bytes 6144 | tf_op jit(solution)/shard_map/gather | solution.py:175
  42.6 3.5 %gather_fusion.7 = f32[512]{0:T(512)S(1)} fusion(f32[512]{0:T(512)S(1)} %fusion.207, s32[1024]{0:T(1024)S(1)} %get-tuple-element.596), kind=kCustom, calls=%fused_computation.7 | custom fusion | bytes 6144 | tf_op jit(solution)/shard_map/gather | solution.py:175
  47.8 1.3 compare_select_fusion.2
  52.9 2.2 %collective-permute-start.2 = (f32[6,18,1,128]{3,2,1,0:T(1,128)S(1)}, f32[6,18,1,128]{3,2,1,0:T(1,128)S(1)}, u32[]{:S(2)}, u32[]{:S(2)}) collective-permute-start(f32[6,18,1,128]{3,2,1,0:T(1,128)S(1)} %get-tuple-element.545), channel_id=1, source_target_pairs={{0,1},{1,2},{2,3},{4,5},{5,6},{6,7},{8,9},{9,10},{10,11},{12,13},{... | collective-permute-start | bytes 165896 | tf_op jit(solution)/shard_map/ppermute | solution.py:27
  55.1 1.3 collective-permute-start.3
  56.8 2.3 %collective-permute-done.3 = f32[6,18,1,128]{3,2,1,0:T(1,128)S(1)} collective-permute-done((f32[6,18,1,128]{3,2,1,0:T(1,128)S(1)}, f32[6,18,1,128]{3,2,1,0:T(1,128)S(1)}, u32[]{:S(2)}, u32[]{:S(2)}) %collective-permute-start.3) | collective-permute-done | bytes 55328 | tf_op jit(solution)/shard_map/ppermute | solution.py:28
  62.5 4.6 %collective-permute-start.4 = (f32[6,1,32,128]{3,2,1,0:T(8,128)S(1)}, f32[6,1,32,128]{3,2,1,0:T(8,128)S(1)}, u32[]{:S(2)}, u32[]{:S(2)}) collective-permute-start(f32[6,1,32,128]{3,2,1,0:T(8,128)S(1)} %get-tuple-element.551), channel_id=1, source_target_pairs={{0,4},{4,8},{8,12},{12,16},{16,20},{20,24},{24,28},{1,5},{5,9},{9,... | collective-permute-start | bytes 294920 | tf_op jit(solution)/shard_map/ppermute | solution.py:27
  67.0 1.3 collective-permute-start.5
  69.6 4.3 %collective-permute-done.5 = f32[6,1,32,128]{3,2,1,0:T(8,128)S(1)} collective-permute-done((f32[6,1,32,128]{3,2,1,0:T(8,128)S(1)}, f32[6,1,32,128]{3,2,1,0:T(8,128)S(1)}, u32[]{:S(2)}, u32[]{:S(2)}) %collective-permute-start.5) | collective-permute-done | bytes 98336 | tf_op jit(solution)/shard_map/ppermute | solution.py:28
  74.0 3.6 %collective-permute-start.6 = (f32[6,18,1,128]{3,2,1,0:T(1,128)S(1)}, f32[6,18,1,128]{3,2,1,0:T(1,128)S(1)}, u32[]{:S(2)}, u32[]{:S(2)}) collective-permute-start(f32[6,18,1,128]{3,2,1,0:T(1,128)S(1)} %get-tuple-element.543), channel_id=1, source_target_pairs={{0,1},{1,2},{2,3},{4,5},{5,6},{6,7},{8,9},{9,10},{10,11},{12,13},{... | collective-permute-start | bytes 165896 | tf_op jit(solution)/shard_map/ppermute | solution.py:27
  77.7 1.3 collective-permute-start.7
  79.3 2.1 %collective-permute-done.7 = f32[6,18,1,128]{3,2,1,0:T(1,128)S(1)} collective-permute-done((f32[6,18,1,128]{3,2,1,0:T(1,128)S(1)}, f32[6,18,1,128]{3,2,1,0:T(1,128)S(1)}, u32[]{:S(2)}, u32[]{:S(2)}) %collective-permute-start.7) | collective-permute-done | bytes 55328 | tf_op jit(solution)/shard_map/ppermute | solution.py:28
  86.1 4.8 %collective-permute-start.8 = (f32[6,1,32,128]{3,2,1,0:T(8,128)S(1)}, f32[6,1,32,128]{3,2,1,0:T(8,128)S(1)}, u32[]{:S(2)}, u32[]{:S(2)}) collective-permute-start(f32[6,1,32,128]{3,2,1,0:T(8,128)S(1)} %get-tuple-element.549), channel_id=1, source_target_pairs={{0,4},{4,8},{8,12},{12,16},{16,20},{20,24},{24,28},{1,5},{5,9},{9,... | collective-permute-start | bytes 294920 | tf_op jit(solution)/shard_map/ppermute | solution.py:27
  90.9 1.3 collective-permute-start.9
  93.1 4.3 %collective-permute-done.9 = f32[6,1,32,128]{3,2,1,0:T(8,128)S(1)} collective-permute-done((f32[6,1,32,128]{3,2,1,0:T(8,128)S(1)}, f32[6,1,32,128]{3,2,1,0:T(8,128)S(1)}, u32[]{:S(2)}, u32[]{:S(2)}) %collective-permute-start.9) | collective-permute-done | bytes 98336 | tf_op jit(solution)/shard_map/ppermute | solution.py:28
  97.5 3.3 %collective-permute-start.10 = (f32[6,18,1,128]{3,2,1,0:T(1,128)S(1)}, f32[6,18,1,128]{3,2,1,0:T(1,128)S(1)}, u32[]{:S(2)}, u32[]{:S(2)}) collective-permute-start(f32[6,18,1,128]{3,2,1,0:T(1,128)S(1)} %get-tuple-element.541), channel_id=1, source_target_pairs={{0,1},{1,2},{2,3},{4,5},{5,6},{6,7},{8,9},{9,10},{10,11},{12,13},{... | collective-permute-start | bytes 165896 | tf_op jit(solution)/shard_map/ppermute | solution.py:27
  100.9 1.5 collective-permute-start.11
  102.7 2.2 %collective-permute-done.11 = f32[6,18,1,128]{3,2,1,0:T(1,128)S(1)} collective-permute-done((f32[6,18,1,128]{3,2,1,0:T(1,128)S(1)}, f32[6,18,1,128]{3,2,1,0:T(1,128)S(1)}, u32[]{:S(2)}, u32[]{:S(2)}) %collective-permute-start.11) | collective-permute-done | bytes 55328 | tf_op jit(solution)/shard_map/ppermute | solution.py:28
  109.1 2.9 %collective-permute-start.12 = (f32[6,1,32,128]{3,2,1,0:T(8,128)S(1)}, f32[6,1,32,128]{3,2,1,0:T(8,128)S(1)}, u32[]{:S(2)}, u32[]{:S(2)}) collective-permute-start(f32[6,1,32,128]{3,2,1,0:T(8,128)S(1)} %get-tuple-element.547), channel_id=1, source_target_pairs={{0,4},{4,8},{8,12},{12,16},{16,20},{20,24},{24,28},{1,5},{5,9},{9,... | collective-permute-start | bytes 294920 | tf_op jit(solution)/shard_map/ppermute | solution.py:27
  112.1 1.3 collective-permute-start.13
  114.3 4.3 %collective-permute-done.13 = f32[6,1,32,128]{3,2,1,0:T(8,128)S(1)} collective-permute-done((f32[6,1,32,128]{3,2,1,0:T(8,128)S(1)}, f32[6,1,32,128]{3,2,1,0:T(8,128)S(1)}, u32[]{:S(2)}, u32[]{:S(2)}) %collective-permute-start.13) | collective-permute-done | bytes 98336 | tf_op jit(solution)/shard_map/ppermute | solution.py:28
  118.7 3.6 %collective-permute-start.14 = (f32[6,18,1,128]{3,2,1,0:T(1,128)S(1)}, f32[6,18,1,128]{3,2,1,0:T(1,128)S(1)}, u32[]{:S(2)}, u32[]{:S(2)}) collective-permute-start(f32[6,18,1,128]{3,2,1,0:T(1,128)S(1)} %get-tuple-element.539), channel_id=1, source_target_pairs={{0,1},{1,2},{2,3},{4,5},{5,6},{6,7},{8,9},{9,10},{10,11},{12,13},{... | collective-permute-start | bytes 165896 | tf_op jit(solution)/shard_map/ppermute | solution.py:27
  122.3 1.3 collective-permute-start.15
  123.9 2.1 %collective-permute-done.15 = f32[6,18,1,128]{3,2,1,0:T(1,128)S(1)} collective-permute-done((f32[6,18,1,128]{3,2,1,0:T(1,128)S(1)}, f32[6,18,1,128]{3,2,1,0:T(1,128)S(1)}, u32[]{:S(2)}, u32[]{:S(2)}) %collective-permute-start.15) | collective-permute-done | bytes 55328 | tf_op jit(solution)/shard_map/ppermute | solution.py:28
  128.4 1.8 fusion.142
  132.9 47.4 %while.29 = (s32[]{:T(128)}, f32[4,16,512]{2,1,0:T(8,128)S(1)}, s32[4]{0:T(128)S(1)}, f32[128]{0:T(128)S(1)}, f32[128]{0:T(128)S(1)}, /*index=5*/f32[16,128]{1,0:T(8,128)S(1)}, s32[]{:T(128)}) while((s32[]{:T(128)}, f32[4,16,512]{2,1,0:T(8,128)S(1)}, s32[4]{0:T(128)S(1)}, f32[128]{0:T(128)S(1)}, f32[128]{0:T(128)S(1)}, ...), condition=%wide.region_7.8_spmd, body=%wide.region_6.7_spmd.sunk | while | flops 27301888 | bytes 438369 | solution.py:226
  134.3 1.3 fusion.276
  135.6 1.3 fusion.277
  136.9 1.3 fusion.278
  138.2 1.3 fusion.279
  139.6 1.3 fusion.274
  140.9 1.3 fusion.275
  142.2 1.3 fusion.272
  143.5 1.3 fusion.273
  146.1 1.3 fusion.276
  147.4 1.3 fusion.277
  148.7 1.3 fusion.278
  150.0 1.3 fusion.279
  151.4 1.3 fusion.274
  152.7 1.3 fusion.275
  154.0 1.3 fusion.272
  155.3 1.3 fusion.273
  159.2 1.3 fusion.277
  160.5 1.3 fusion.278
  161.8 1.3 fusion.279
  164.5 1.3 fusion.275
  165.8 1.3 fusion.272
  167.1 1.3 fusion.273
  171.0 1.3 fusion.277
  172.3 1.3 fusion.278
  173.6 1.3 fusion.279
  176.3 1.3 fusion.275
  177.6 1.3 fusion.272
  178.9 1.3 fusion.273
  181.3 17.1 %all_to_all.6 = f32[32,4,512]{2,1,0:T(4,128)S(1)} all-to-all(f32[32,4,512]{2,1,0:T(4,128)S(1)} %copy.611), channel_id=1, replica_groups=mesh['gx'=8,'gy'=4] {'gx','gy'}, dimensions={0} | all-to-all | bytes 524288 | tf_op jit(solution)/shard_map/all_to_all | solution.py:233
  (244 shorter events, 43.2 us)
Async XLA Ops:
  0.6 8.6 %copy-start.7 = (f32[2,128]{1,0:T(2,128)S(1)}, f32[2,128]{1,0:T(2,128)}, u32[]{:S(2)}) copy-start(f32[2,128]{1,0:T(2,128)} %param.56) | copy-start | bytes 3076
  3.0 49.7 %collective-permute-start = (f32[6,1,32,128]{3,2,1,0:T(8,128)S(1)}, f32[6,1,32,128]{3,2,1,0:T(8,128)S(1)}, u32[]{:S(2)}, u32[]{:S(2)}) collective-permute-start(f32[6,1,32,128]{3,2,1,0:T(8,128)S(1)} %get-tuple-element.553), channel_id=1, source_target_pairs={{0,4},{4,8},{8,12},{12,16},{16,20},{20,24},{24,28},{1,5},{5,9},{9,... | collective-permute-start | bytes 294920 | tf_op jit(solution)/shard_map/ppermute | solution.py:27
  7.9 44.9 %collective-permute-start.1 = (f32[6,1,32,128]{3,2,1,0:T(8,128)S(1)}, f32[6,1,32,128]{3,2,1,0:T(8,128)S(1)}, u32[]{:S(2)}, u32[]{:S(2)}) collective-permute-start(f32[6,1,32,128]{3,2,1,0:T(8,128)S(1)} %get-tuple-element.554), channel_id=1, source_target_pairs={{4,0},{8,4},{12,8},{16,12},{20,16},{24,20},{28,24},{5,1},{9,5},{13... | collective-permute-start | bytes 294920 | tf_op jit(solution)/shard_map/ppermute | solution.py:28
  27.1 4.3 %copy-start.12 = (s32[1,1,128]{2,1,0:T(1,128)S(1)}, s32[1,1,128]{2,1,0:T(1,128)}, u32[]{:S(2)}) copy-start(s32[1,1,128]{2,1,0:T(1,128)} %param.58) | copy-start | bytes 1540
  42.5 4.5 %copy-start.13 = (s32[64]{0:T(128)S(1)}, s32[64]{0:T(128)}, u32[]{:S(2)}) copy-start(s32[64]{0:T(128)} %param.59) | copy-start | bytes 772
  42.5 4.7 %copy-start.6 = (s32[8,4]{0,1:T(4,128)S(1)}, s32[8,4]{0,1:T(4,128)}, u32[]{:S(2)}) copy-start(s32[8,4]{0,1:T(4,128)} %param.57) | copy-start | bytes 388
  42.5 7.3 %copy-start.14 = (s32[5]{0:T(128)S(1)}, s32[5]{0:T(128)}, u32[]{:S(2)}) copy-start(s32[5]{0:T(128)} %constant.568.clone.1) | copy-start | bytes 64
  42.5 9.5 %copy-start.5 = (s32[16,32,128]{2,1,0:T(8,128)S(1)}, s32[16,32,128]{2,1,0:T(8,128)}, u32[]{:S(2)}) copy-start(s32[16,32,128]{2,1,0:T(8,128)} %param.51) | copy-start | bytes 786436
  42.5 9.5 %copy-start.8 = (f32[8]{0:T(128)S(1)}, f32[8]{0:T(128)}, u32[]{:S(2)}) copy-start(f32[8]{0:T(128)} %param.53) | copy-start | bytes 100
  42.5 9.5 %copy-start.9 = (f32[8]{0:T(128)S(1)}, f32[8]{0:T(128)}, u32[]{:S(2)}) copy-start(f32[8]{0:T(128)} %param.55) | copy-start | bytes 100
  42.6 9.5 %copy-start.10 = (f32[8]{0:T(128)S(1)}, f32[8]{0:T(128)}, u32[]{:S(2)}) copy-start(f32[8]{0:T(128)} %param.54) | copy-start | bytes 100
  42.6 9.5 %copy-start.11 = (f32[8]{0:T(128)S(1)}, f32[8]{0:T(128)}, u32[]{:S(2)}) copy-start(f32[8]{0:T(128)} %param.52) | copy-start | bytes 100
  52.9 3.6 %collective-permute-start.2 = (f32[6,18,1,128]{3,2,1,0:T(1,128)S(1)}, f32[6,18,1,128]{3,2,1,0:T(1,128)S(1)}, u32[]{:S(2)}, u32[]{:S(2)}) collective-permute-start(f32[6,18,1,128]{3,2,1,0:T(1,128)S(1)} %get-tuple-element.545), channel_id=1, source_target_pairs={{0,1},{1,2},{2,3},{4,5},{5,6},{6,7},{8,9},{9,10},{10,11},{12,13},{... | collective-permute-start | bytes 165896 | tf_op jit(solution)/shard_map/ppermute | solution.py:27
  55.1 4.0 %collective-permute-start.3 = (f32[6,18,1,128]{3,2,1,0:T(1,128)S(1)}, f32[6,18,1,128]{3,2,1,0:T(1,128)S(1)}, u32[]{:S(2)}, u32[]{:S(2)}) collective-permute-start(f32[6,18,1,128]{3,2,1,0:T(1,128)S(1)} %get-tuple-element.546), channel_id=1, source_target_pairs={{1,0},{2,1},{3,2},{5,4},{6,5},{7,6},{9,8},{10,9},{11,10},{13,12},{... | collective-permute-start | bytes 165896 | tf_op jit(solution)/shard_map/ppermute | solution.py:28
  60.4 1.1 copy-start.2
  60.4 1.4 copy-start.3
  62.5 7.2 %collective-permute-start.4 = (f32[6,1,32,128]{3,2,1,0:T(8,128)S(1)}, f32[6,1,32,128]{3,2,1,0:T(8,128)S(1)}, u32[]{:S(2)}, u32[]{:S(2)}) collective-permute-start(f32[6,1,32,128]{3,2,1,0:T(8,128)S(1)} %get-tuple-element.551), channel_id=1, source_target_pairs={{0,4},{4,8},{8,12},{12,16},{16,20},{20,24},{24,28},{1,5},{5,9},{9,... | collective-permute-start | bytes 294920 | tf_op jit(solution)/shard_map/ppermute | solution.py:27
  67.0 6.9 %collective-permute-start.5 = (f32[6,1,32,128]{3,2,1,0:T(8,128)S(1)}, f32[6,1,32,128]{3,2,1,0:T(8,128)S(1)}, u32[]{:S(2)}, u32[]{:S(2)}) collective-permute-start(f32[6,1,32,128]{3,2,1,0:T(8,128)S(1)} %get-tuple-element.552), channel_id=1, source_target_pairs={{4,0},{8,4},{12,8},{16,12},{20,16},{24,20},{28,24},{5,1},{9,5},{13... | collective-permute-start | bytes 294920 | tf_op jit(solution)/shard_map/ppermute | solution.py:28
  74.0 4.9 %collective-permute-start.6 = (f32[6,18,1,128]{3,2,1,0:T(1,128)S(1)}, f32[6,18,1,128]{3,2,1,0:T(1,128)S(1)}, u32[]{:S(2)}, u32[]{:S(2)}) collective-permute-start(f32[6,18,1,128]{3,2,1,0:T(1,128)S(1)} %get-tuple-element.543), channel_id=1, source_target_pairs={{0,1},{1,2},{2,3},{4,5},{5,6},{6,7},{8,9},{9,10},{10,11},{12,13},{... | collective-permute-start | bytes 165896 | tf_op jit(solution)/shard_map/ppermute | solution.py:27
  77.7 3.8 %collective-permute-start.7 = (f32[6,18,1,128]{3,2,1,0:T(1,128)S(1)}, f32[6,18,1,128]{3,2,1,0:T(1,128)S(1)}, u32[]{:S(2)}, u32[]{:S(2)}) collective-permute-start(f32[6,18,1,128]{3,2,1,0:T(1,128)S(1)} %get-tuple-element.544), channel_id=1, source_target_pairs={{1,0},{2,1},{3,2},{5,4},{6,5},{7,6},{9,8},{10,9},{11,10},{13,12},{... | collective-permute-start | bytes 165896 | tf_op jit(solution)/shard_map/ppermute | solution.py:28
  82.8 1.1 copy-start
  86.1 7.0 %collective-permute-start.8 = (f32[6,1,32,128]{3,2,1,0:T(8,128)S(1)}, f32[6,1,32,128]{3,2,1,0:T(8,128)S(1)}, u32[]{:S(2)}, u32[]{:S(2)}) collective-permute-start(f32[6,1,32,128]{3,2,1,0:T(8,128)S(1)} %get-tuple-element.549), channel_id=1, source_target_pairs={{0,4},{4,8},{8,12},{12,16},{16,20},{20,24},{24,28},{1,5},{5,9},{9,... | collective-permute-start | bytes 294920 | tf_op jit(solution)/shard_map/ppermute | solution.py:27
  90.9 6.5 %collective-permute-start.9 = (f32[6,1,32,128]{3,2,1,0:T(8,128)S(1)}, f32[6,1,32,128]{3,2,1,0:T(8,128)S(1)}, u32[]{:S(2)}, u32[]{:S(2)}) collective-permute-start(f32[6,1,32,128]{3,2,1,0:T(8,128)S(1)} %get-tuple-element.550), channel_id=1, source_target_pairs={{4,0},{8,4},{12,8},{16,12},{20,16},{24,20},{28,24},{5,1},{9,5},{13... | collective-permute-start | bytes 294920 | tf_op jit(solution)/shard_map/ppermute | solution.py:28
  97.5 4.8 %collective-permute-start.10 = (f32[6,18,1,128]{3,2,1,0:T(1,128)S(1)}, f32[6,18,1,128]{3,2,1,0:T(1,128)S(1)}, u32[]{:S(2)}, u32[]{:S(2)}) collective-permute-start(f32[6,18,1,128]{3,2,1,0:T(1,128)S(1)} %get-tuple-element.541), channel_id=1, source_target_pairs={{0,1},{1,2},{2,3},{4,5},{5,6},{6,7},{8,9},{9,10},{10,11},{12,13},{... | collective-permute-start | bytes 165896 | tf_op jit(solution)/shard_map/ppermute | solution.py:27
  100.9 4.0 %collective-permute-start.11 = (f32[6,18,1,128]{3,2,1,0:T(1,128)S(1)}, f32[6,18,1,128]{3,2,1,0:T(1,128)S(1)}, u32[]{:S(2)}, u32[]{:S(2)}) collective-permute-start(f32[6,18,1,128]{3,2,1,0:T(1,128)S(1)} %get-tuple-element.542), channel_id=1, source_target_pairs={{1,0},{2,1},{3,2},{5,4},{6,5},{7,6},{9,8},{10,9},{11,10},{13,12},{... | collective-permute-start | bytes 165896 | tf_op jit(solution)/shard_map/ppermute | solution.py:28
  109.1 5.1 %collective-permute-start.12 = (f32[6,1,32,128]{3,2,1,0:T(8,128)S(1)}, f32[6,1,32,128]{3,2,1,0:T(8,128)S(1)}, u32[]{:S(2)}, u32[]{:S(2)}) collective-permute-start(f32[6,1,32,128]{3,2,1,0:T(8,128)S(1)} %get-tuple-element.547), channel_id=1, source_target_pairs={{0,4},{4,8},{8,12},{12,16},{16,20},{20,24},{24,28},{1,5},{5,9},{9,... | collective-permute-start | bytes 294920 | tf_op jit(solution)/shard_map/ppermute | solution.py:27
  112.1 6.5 %collective-permute-start.13 = (f32[6,1,32,128]{3,2,1,0:T(8,128)S(1)}, f32[6,1,32,128]{3,2,1,0:T(8,128)S(1)}, u32[]{:S(2)}, u32[]{:S(2)}) collective-permute-start(f32[6,1,32,128]{3,2,1,0:T(8,128)S(1)} %get-tuple-element.548), channel_id=1, source_target_pairs={{4,0},{8,4},{12,8},{16,12},{20,16},{24,20},{28,24},{5,1},{9,5},{13... | collective-permute-start | bytes 294920 | tf_op jit(solution)/shard_map/ppermute | solution.py:28
  118.7 4.9 %collective-permute-start.14 = (f32[6,18,1,128]{3,2,1,0:T(1,128)S(1)}, f32[6,18,1,128]{3,2,1,0:T(1,128)S(1)}, u32[]{:S(2)}, u32[]{:S(2)}) collective-permute-start(f32[6,18,1,128]{3,2,1,0:T(1,128)S(1)} %get-tuple-element.539), channel_id=1, source_target_pairs={{0,1},{1,2},{2,3},{4,5},{5,6},{6,7},{8,9},{9,10},{10,11},{12,13},{... | collective-permute-start | bytes 165896 | tf_op jit(solution)/shard_map/ppermute | solution.py:27
  122.3 3.8 %collective-permute-start.15 = (f32[6,18,1,128]{3,2,1,0:T(1,128)S(1)}, f32[6,18,1,128]{3,2,1,0:T(1,128)S(1)}, u32[]{:S(2)}, u32[]{:S(2)}) collective-permute-start(f32[6,18,1,128]{3,2,1,0:T(1,128)S(1)} %get-tuple-element.540), channel_id=1, source_target_pairs={{1,0},{2,1},{3,2},{5,4},{6,5},{7,6},{9,8},{10,9},{11,10},{13,12},{... | collective-permute-start | bytes 165896 | tf_op jit(solution)/shard_map/ppermute | solution.py:28
  127.2 0.9 copy-start.1
  130.2 2.7 %copy-start.4 = (f32[3,16,32,128]{3,2,1,0:T(8,128)}, f32[3,16,32,128]{3,2,1,0:T(8,128)S(1)}, u32[]{:S(2)}) copy-start(f32[3,16,32,128]{3,2,1,0:T(8,128)S(1)} %get-tuple-element.504) | copy-start | bytes 2359300
where the time goes:
time: 200 us; the launch traced here: 199 us
  local copies, waits for them, and re-layouts  45.4 us (23%)
  matrix products  41.7 us (21%)
  starting transfers between devices  40.4 us (20%)
  other arithmetic  23.5 us (12%)
  waiting for transfers between devices  23.5 us (12%)
  blocking collectives  22.2 us (11%)
    ppermute x8, starting transfers between devices, extended(): before = lax.ppermute(last, axis, up)  29.9 us
    ppermute x8, waiting for transfers between devices, extended(): after = lax.ppermute(leading, axis, down)  21.8 us
    all_to_all x1, blocking collectives, shards(): lax.all_to_all(placed, ('gx', 'gy'), split_axis=0, concat_axis=0, tiled=T...  17.1 us
    gather x8, local copies, waits for them, and re-layouts, shards(): inject_e = e_line[inject_index] * region_mask  16.2 us
    gather x8, local copies, waits for them, and re-layouts, shards(): inject_h = h_line[inject_index[1:, 1:]] * region_mask[1:, 1:]  14.3 us
    ppermute x8, starting transfers between devices, extended(): after = lax.ppermute(leading, axis, down)  10.5 us
    dot_general x8, matrix products, radiate(): jnp.dot(real_rows, sine_part.T, precision=HIGHEST)  10.4 us
    dot_general x8, matrix products, radiate(): jnp.dot(imag_rows, sine_part.T, precision=HIGHEST)  10.4 us
  transfers between devices with their start and end apart: 16, of which 9 were waited for; matrix products, arithmetic and copies ran while one was open for 20% of the time, Pallas kernels for 0%

commit v1 on v0

v1 whole, which is shorter than its diff:
```python
import functools
import math

import jax
import jax.numpy as jnp
import numpy as np
from jax import lax
from jax.experimental import pallas as pl
from jax.experimental.pallas import tpu as pltpu
from jax.sharding import PartitionSpec as P

STEPS = 4
NF = 2
DB = 32
BMAX = 4
FREQS = (0.35, 0.6)
WAVENUMS = (0.7, 1.2)
COURANT = 0.5
HIGHEST = lax.Precision.HIGHEST
MESH = pl.DeviceIdType.MESH
PAD = 8


def phase_tables(gx_n, gy_n, cx, cy, total_dirs):
    nu = 64
    nv = total_dirs // nu
    u = (np.arange(nu) + 0.5) / 32.0 - 1.0
    v = (np.arange(nv) + 0.5) * (128.0 / total_dirs) - 1.0
    ys = np.arange(gy_n * cy).reshape(gy_n, cy)
    xs = np.arange(gx_n * cx)
    vt = np.zeros((gy_n, NF, 2 * nv, cy), np.float32)
    wt = np.zeros((NF, gx_n * cx, 2 * nu), np.float32)
    for f, k in enumerate(WAVENUMS):
        ph = k * v[None, :, None] * ys[:, None, :]
        vt[:, f, :nv] = np.cos(ph)
        vt[:, f, nv:] = np.sin(ph)
        pu = k * xs[:, None] * u[None, :]
        wt[f, :, :nu] = np.cos(pu)
        wt[f, :, nu:] = np.sin(pu)
    return vt, wt


def kernel_body(
    dims,
    mask_s,
    owner_s,
    ieps_s,
    dec_s,
    drv_s,
    res_s,
    e_in,
    h_in,
    j_in,
    p_in,
    mat_in,
    line_in,
    slots_in,
    vt_in,
    wt_in,
    e_out,
    h_out,
    j_out,
    p_out,
    far_out,
    e, h, j, p, mat, coef, line_b, line_o, slots, vt, wt,
    xm, xp, ym, yp, ca, cb, ys1, ys0, cas, cbs, hys, gxh, gyh,
    col_e, col_h, ssum, tsend, trecv, tsr, msend, mall, far,
    in_sem, out_sem, snd, rcv, gsnd, grcv, lsnd, lrcv, fsnd, frcv,
):
    GX, GY, X, Y, Z, NB = dims
    N = GX * GY
    V = N
    c = COURANT
    gx = lax.axis_index("gx")
    gy = lax.axis_index("gy")
    me = gx * GY + gy

    loads = [
        pltpu.make_async_copy(e_in, e.at[:, pl.ds(0, X)], in_sem.at[0]),
        pltpu.make_async_copy(h_in, h, in_sem.at[1]),
        pltpu.make_async_copy(line_in, line_o, in_sem.at[2]),
        pltpu.make_async_copy(mat_in, mat, in_sem.at[3]),
        pltpu.make_async_copy(j_in, j, in_sem.at[4]),
        pltpu.make_async_copy(p_in, p, in_sem.at[5]),
        pltpu.make_async_copy(slots_in, slots, in_sem.at[6]),
        pltpu.make_async_copy(vt_in.at[gy], vt, in_sem.at[7]),
        pltpu.make_async_copy(wt_in, wt, in_sem.at[8]),
    ]
    for cp in loads:
        cp.start()

    has_xm, has_xp = gx > 0, gx < GX - 1
    has_ym, has_yp = gy > 0, gy < GY - 1

    @pl.when(gx == 0)
    def _():
        xm[...] = jnp.zeros_like(xm)
        gxh[...] = jnp.zeros_like(gxh)

    @pl.when(gx == GX - 1)
    def _():
        xp[...] = jnp.zeros_like(xp)

    @pl.when(gy == 0)
    def _():
        ym[...] = jnp.zeros_like(ym)
        gyh[...] = jnp.zeros_like(gyh)

    @pl.when(gy == GY - 1)
    def _():
        yp[...] = jnp.zeros_like(yp)

    @pl.when((gx == 0) | (gy == GY - 1))
    def _():
        ca[...] = jnp.zeros_like(ca)

    @pl.when((gx == GX - 1) | (gy == 0))
    def _():
        cb[...] = jnp.zeros_like(cb)

    barrier = pltpu.get_barrier_semaphore()

    def greet(i, carry):
        d = lax.rem(me + i, N)
        pl.semaphore_signal(barrier, inc=1, device_id=(d // GY, lax.rem(d, GY)), device_id_type=MESH)
        return carry

    lax.fori_loop(1, N, greet, 0)

    loads[0].wait()
    loads[1].wait()

    def pack(x, carry):
        r = pl.ds(x, 1)
        for k in range(3):
            ys1[k, r, :] = e[k, x, pl.ds(Y - 1, 1), :]
        ys0[0, r, :] = e[0, x, pl.ds(0, 1), :]
        ys0[1, r, :] = e[2, x, pl.ds(0, 1), :]
        hys[0, r, :] = h[0, x, pl.ds(Y - 1, 1), :]
        hys[1, r, :] = h[2, x, pl.ds(Y - 1, 1), :]
        return carry

    lax.fori_loop(0, X, pack, 0)
    cas[...] = e[0, X - 1, pl.ds(0, 1), :]
    cbs[...] = e[1, 0, pl.ds(Y - 1, 1), :]
    loads[2].wait()

    pl.semaphore_wait(barrier, N - 1)

    def remote(src, dst, s, r, dx, dy):
        return pltpu.make_async_remote_copy(
            src_ref=src, dst_ref=dst, send_sem=s, recv_sem=r,
            device_id=(gx + dx, gy + dy), device_id_type=MESH,
        )

    def halo(n):
        def cp(src, dst, k, dx, dy):
            return remote(src, dst, snd.at[n, k], rcv.at[n, k], dx, dy)

        return [
            (has_xp, has_xm, cp(e.at[:, X - 1], xm.at[n], 0, 1, 0)),
            (has_xm, has_xp, cp(e.at[pl.ds(1, 2), 0], xp.at[n], 1, -1, 0)),
            (has_yp, has_ym, cp(ys1, ym.at[n], 2, 0, 1)),
            (has_ym, has_yp, cp(ys0, yp.at[n], 3, 0, -1)),
            (has_xp & has_ym, has_xm & has_yp, cp(cas, ca.at[n], 4, 1, -1)),
            (has_xm & has_yp, has_xp & has_ym, cp(cbs, cb.at[n], 5, -1, 1)),
        ]

    first_h = [
        (has_xp, has_xm, remote(h.at[pl.ds(1, 2), X - 1], gxh, gsnd.at[0], grcv.at[0], 1, 0)),
        (has_yp, has_ym, remote(hys, gyh, gsnd.at[1], grcv.at[1], 0, 1)),
    ]
    line_cp = []
    for q in range(1, GY):
        dst_gy = lax.rem(gy + q, GY)
        line_cp.append(
            pltpu.make_async_remote_copy(
                src_ref=line_o, dst_ref=line_b.at[gy], send_sem=lsnd.at[q],
                recv_sem=lrcv.at[q], device_id=(gx, dst_gy), device_id_type=MESH,
            )
        )

    def start(copies):
        for to, _, cp in copies:
            pl.when(to)(cp.start)

    def finish(copies):
        for to, frm, cp in copies:
            pl.when(frm)(cp.wait_recv)
            pl.when(to)(cp.wait_send)

    halo0 = halo(0)
    start(halo0)
    start(first_h)
    for cp in line_cp:
        cp.start()
    line_b[gy] = line_o[...]

    lane = lax.broadcasted_iota(jnp.int32, (Y, Z), 1)
    row = lax.broadcasted_iota(jnp.int32, (Y, Z), 0)
    lane_x = lax.broadcasted_iota(jnp.int32, (X, Z), 1)
    row_x = lax.broadcasted_iota(jnp.int32, (X, Z), 0)
    z_h = Z // 4 - 1
    z_e = Z // 4
    z_s = Z // 4 - 3

    loads[3].wait()

    def table(x, carry):
        m = mat[x]
        outs = [jnp.full((Y, Z), t[0], jnp.float32) for t in (ieps_s, dec_s, drv_s, res_s)]
        for k in range(1, 8):
            hit = m == k
            outs = [jnp.where(hit, t[k], o) for t, o in zip((ieps_s, dec_s, drv_s, res_s), outs)]
        for k in range(4):
            coef[k, x] = outs[k]
        return carry

    lax.fori_loop(0, X, table, 0)

    loads[6].wait()
    sl = slots[...]
    sl_pos = jnp.maximum(sl, 0)
    sl_x = sl_pos // Y
    sl_y = sl_pos - sl_x * Y
    L = sl.shape[-1]
    one_y = ((lax.broadcasted_iota(jnp.int32, (Y, L), 0) == sl_y) & (sl >= 0)).astype(jnp.bfloat16)
    one_x = (lax.rem(lax.broadcasted_iota(jnp.int32, (128, L), 0), X) == sl_x).astype(jnp.bfloat16)
    cell_mask = lax.dot_general(
        one_y, one_x, (((1,), (1,)), ((), ())), preferred_element_type=jnp.float32
    )

    def mine(b, carry):
        cnt, b0, b1, b2, b3 = carry
        hit = owner_s[b] == me
        b0 = jnp.where(hit & (cnt == 0), b, b0)
        b1 = jnp.where(hit & (cnt == 1), b, b1)
        b2 = jnp.where(hit & (cnt == 2), b, b2)
        b3 = jnp.where(hit & (cnt == 3), b, b3)
        return cnt + hit.astype(jnp.int32), b0, b1, b2, b3

    neg = jnp.int32(-1)
    picks = lax.fori_loop(0, NB, mine, (jnp.int32(0), neg, neg, neg, neg))[1:]

    loads[4].wait()
    loads[5].wait()
    for cp in line_cp:
        cp.wait()

    LL = line_o.shape[1]
    R = col_e.shape[1]
    base = gx * X + gy * Y - PAD
    target = 2 * (base + lax.broadcasted_iota(jnp.int32, (R, LL), 0))
    where_l = lax.broadcasted_iota(jnp.int32, (R, LL), 1)
    acc = [jnp.zeros((R, LL), jnp.float32) for _ in range(4)]
    for q in range(GY):
        for par in range(2):
            hit = target + par == where_l + q * LL
            for k in range(2):
                acc[2 * k + par] += jnp.where(hit, line_b[q, pl.ds(k, 1), :], 0.0)
    cols = [jnp.broadcast_to(jnp.sum(a, axis=1, keepdims=True), (R, Z)) for a in acc]
    ev, od, hv, ho = cols
    t2 = 2 * (base + lax.broadcasted_iota(jnp.int32, (R, Z), 0))
    keep_v = ((t2 >= 0) & (t2 < GY * LL)).astype(jnp.float32)
    for n in range(STEPS):
        col_e[n] = od
        ho = (ho - c * (pltpu.roll(ev, R - 1, 0) - od)) * keep_v
        hv = (hv - c * (od - ev)) * keep_v
        col_h[n] = ho
        ev = (ev - c * (hv - pltpu.roll(ho, 1, 0))) * keep_v
        od = (od - c * (ho - hv)) * keep_v

    m_own = mask_s[gx, gy].astype(jnp.float32)
    m_left = mask_s[jnp.maximum(gx - 1, 0), gy].astype(jnp.float32)
    keep_x = has_xm.astype(jnp.float32)
    keep_y = has_ym.astype(jnp.float32)

    def fz(v, ln):
        return jnp.where(ln == Z - 1, 0.0, pltpu.roll(v, Z - 1, 1)) - v

    def bz(v):
        return v - jnp.where(lane == 0, 0.0, pltpu.roll(v, 1, 1))

    def up_y(v, edge):
        return jnp.where(row == Y - 1, edge, pltpu.roll(v, Y - 1, 0))

    def down_y(v, edge):
        return jnp.where(row == 0, edge, pltpu.roll(v, 1, 0))

    finish(first_h)
    for n in range(STEPS):
        finish(halo0 if n == 0 else pending)
        e[1, X] = xp[n, 0]
        e[2, X] = xp[n, 1]
        ex_m, ey_m, ez_m = xm[n, 0], xm[n, 1], xm[n, 2]
        inj = jnp.where(lane == z_h, (c * m_left) * col_e[n, pl.ds(PAD - 1, Y), :], 0.0)
        gh_y = gxh[0] - c * (fz(ex_m, lane) - (e[2, 0] - ez_m)) + inj
        gh_z = gxh[1] - c * ((e[1, 0] - ey_m) - (up_y(ex_m, ca[n]) - ex_m))
        gh_y = gh_y * keep_x
        gh_z = gh_z * keep_x
        gxh[0] = gh_y
        gxh[1] = gh_z
        ex_m, ey_m, ez_m = ym[n, 0], ym[n, 1], ym[n, 2]
        ey_next = jnp.where(row_x == X - 1, cb[n], pltpu.roll(ey_m, X - 1, 0))
        gyh[0] = (gyh[0] - c * ((ys0[1] - ez_m) - fz(ey_m, lane_x))) * keep_y
        gyh[1] = (gyh[1] - c * ((ey_next - ey_m) - (ys0[0] - ex_m))) * keep_y

        def step(x, carry, n=n):
            hy_m, hz_m, plane = carry
            r = pl.ds(x, 1)
            ex, ey, ez = e[0, x], e[1, x], e[2, x]
            ey_x, ez_x = e[1, x + 1], e[2, x + 1]
            hx = h[0, x] - c * ((up_y(ez, yp[n, 1, r, :]) - ez) - fz(ey, lane))
            inj_e = jnp.where(lane == z_h, (c * m_own) * col_e[n, pl.ds(x + PAD, Y), :], 0.0)
            hy = h[1, x] - c * (fz(ex, lane) - (ez_x - ez)) + inj_e
            hz = h[2, x] - c * ((ey_x - ey) - (up_y(ex, yp[n, 0, r, :]) - ex))
            h[0, x] = hx
            h[1, x] = hy
            h[2, x] = hz
            inj_h = jnp.where(lane == z_e, m_own * col_h[n, pl.ds(x + PAD, Y), :], 0.0)
            cx = (hz - down_y(hz, gyh[1, r, :])) - bz(hy) + inj_h
            cy = bz(hx) - (hz - hz_m)
            cz = (hy - hy_m) - (hx - down_y(hx, gyh[0, r, :]))
            ie, dc, dr, rs = coef[0, x], coef[1, x], coef[2, x], coef[3, x]
            new = []
            for k, (old, curl) in enumerate(((ex, cx), (ey, cy), (ez, cz))):
                jo = j[k, x]
                po = p[k, x]
                en = old + ie * (c * curl - jo)
                jn = dc * jo + dr * en - rs * po
                e[k, x] = en
                j[k, x] = jn
                p[k, x] = po + jn
                new.append(en)
            if n < STEPS - 1:
                for k in range(3):
                    ys1[k, r, :] = new[k][Y - 1 : Y]
                ys0[0, r, :] = new[0][0:1]
                ys0[1, r, :] = new[2][0:1]
            l64 = lax.rem(lane, 4 * X)
            for k, val in enumerate((new[0], new[1], hx, hy)):
                plane = jnp.where(l64 == k * X + x, val[:, z_s : z_s + 1], plane)
            return hy, hz, plane

        zero = jnp.zeros((Y, Z), jnp.float32)
        plane = lax.fori_loop(0, X, step, (gh_y, gh_z, zero))[2]
        if n < STEPS - 1:
            cas[...] = e[0, X - 1, pl.ds(0, 1), :]
            cbs[...] = e[1, 0, pl.ds(Y - 1, 1), :]
            pending = halo(n + 1)
            start(pending)
        for f in range(NF):
            wc = math.cos(FREQS[f] * (n + 1))
            ws = -math.sin(FREQS[f] * (n + 1))
            add = jnp.where(lane < 4 * X, wc, ws) * plane
            ssum[f] = add if n == 0 else ssum[f] + add

    stores = [
        pltpu.make_async_copy(e.at[:, pl.ds(0, X)], e_out, out_sem.at[0]),
        pltpu.make_async_copy(h, h_out, out_sem.at[1]),
        pltpu.make_async_copy(j, j_out, out_sem.at[2]),
        pltpu.make_async_copy(p, p_out, out_sem.at[3]),
    ]
    for cp in stores:
        cp.start()

    loads[7].wait()
    loads[8].wait()
    lane_v = lax.broadcasted_iota(jnp.int32, (V, 128), 1)
    for f in range(NF):
        cd = jnp.dot(vt[f], ssum[f] * cell_mask, precision=HIGHEST, preferred_element_type=jnp.float32)
        turned = pltpu.roll(cd[V:], 64, 1)
        t = cd[:V] + jnp.where(lane_v < 64, -turned, turned)
        for v in range(V):
            tsend[v, pl.ds(f, 1), :] = t[v : v + 1]

    def send_t(i, carry):
        d = lax.rem(me + i, N)
        pltpu.make_async_remote_copy(
            src_ref=tsend.at[d], dst_ref=trecv.at[me], send_sem=fsnd.at[0], recv_sem=frcv.at[0],
            device_id=(d // GY, lax.rem(d, GY)), device_id_type=MESH,
        ).start()
        return carry

    lax.fori_loop(1, N, send_t, 0)
    trecv[me] = tsend[me]
    part = pl.ds(0, N - 1)
    pltpu.make_async_copy(trecv.at[part], trecv.at[part], frcv.at[0]).wait()

    for q in range(GX):
        total = trecv[q * GY]
        for s in range(1, GY):
            total = total + trecv[q * GY + s]
        for f in range(NF):
            tsr[f, pl.ds(q, 1), :] = total[f : f + 1]

    l8 = lax.broadcasted_iota(jnp.int32, (8, 128), 1)
    r8 = lax.broadcasted_iota(jnp.int32, (8, 128), 0)
    blk = l8 // X
    grp = l8 // 32
    rows_out = [None] * 8
    for f in range(NF):
        g = jnp.zeros((8, 128), jnp.float32)
        for o in range(GX // 8):
            a = tsr[f, pl.ds(8 * o, 8), :]
            for s in (4, 2, 1):
                from_down = pltpu.roll(pltpu.roll(a, 8 - s, 0), X * s, 1)
                from_up = pltpu.roll(pltpu.roll(a, s, 0), 128 - X * s, 1)
                bi = (r8 & s) != 0
                bj = (blk & s) != 0
                a = jnp.where(bi == bj, a, jnp.where(bj, from_down, from_up))
            g = g + jnp.dot(a, wt[f, pl.ds(o * 128, 128), :], precision=HIGHEST,
                            preferred_element_type=jnp.float32)
        for hh in range(2):
            rep = []
            for cs in range(2):
                w = jnp.where(grp == cs * 2 + hh, g, 0.0)
                w = w + pltpu.roll(w, 32, 1)
                rep.append(w + pltpu.roll(w, 64, 1))
            for chi in range(2):
                comp = chi * 2 + grp // 2
                part_b = grp & 1
                same = r8 == part_b * 4 + comp
                other = r8 == (1 - part_b) * 4 + comp
                sgn = jnp.where(part_b == 1, 1.0, -1.0)
                mix = jnp.where(same, rep[0], 0.0) + jnp.where(other, sgn * rep[1], 0.0)
                rows_out[hh * 4 + f * 2 + chi] = jnp.sum(mix, axis=0, keepdims=True)
    scale = 1.0 / math.sqrt(N * L)
    for i in range(8):
        msend[pl.ds(i, 1), :] = rows_out[i] * scale

    def send_m(i, carry):
        d = lax.rem(me + i, N)
        pltpu.make_async_remote_copy(
            src_ref=msend, dst_ref=mall.at[me], send_sem=fsnd.at[1], recv_sem=frcv.at[1],
            device_id=(d // GY, lax.rem(d, GY)), device_id_type=MESH,
        ).start()
        return carry

    lax.fori_loop(1, N, send_m, 0)
    mall[me] = msend[...]
    pltpu.make_async_copy(mall.at[part], mall.at[part], frcv.at[1]).wait()
    for r in range(BMAX):
        b = picks[r]
        ok = (b >= 0).astype(jnp.float32)
        bb = jnp.maximum(b, 0)
        tile = mall[bb // 2] * ok
        half = jnp.where(lax.rem(bb, 2) == 1, tile[4:8], tile[0:4])
        for k in range(4):
            far[pl.ds(r, 1), pl.ds(k * 128, 128)] = half[k : k + 1]
    last = pltpu.make_async_copy(far, far_out, out_sem.at[4])
    last.start()
    pltpu.make_async_copy(tsend.at[part], tsend.at[part], fsnd.at[0]).wait()
    pltpu.make_async_copy(mall.at[part], mall.at[part], fsnd.at[1]).wait()
    for cp in stores:
        cp.wait()
    last.wait()


def shards(e, h, jc, pz, mat, ieps, dec, drv, res, line, mask, slots, owner, gx_n=0, gy_n=0):
    _, X, Y, Z = e.shape
    N = gx_n * gy_n
    NB = owner.shape[0]
    vt, wt = phase_tables(gx_n, gy_n, X, Y, NB * DB)
    f32 = jnp.float32
    any_spec = pl.BlockSpec(memory_space=pl.ANY)
    smem = pl.BlockSpec(memory_space=pltpu.SMEM)
    field = jax.ShapeDtypeStruct((3, X, Y, Z), f32)
    rows = X + Y + 2 * PAD
    VM = pltpu.VMEM
    dma = pltpu.SemaphoreType.DMA
    scratch = [
        VM((3, X + 1, Y, Z), f32), VM((3, X, Y, Z), f32), VM((3, X, Y, Z), f32),
        VM((3, X, Y, Z), f32), VM((X, Y, Z), jnp.int32), VM((4, X, Y, Z), f32),
        VM((gy_n,) + line.shape, f32), VM(line.shape, f32), VM((1, slots.shape[-1]), jnp.int32),
        VM(vt.shape[1:], f32), VM(wt.shape, f32),
        VM((STEPS, 3, Y, Z), f32), VM((STEPS, 2, Y, Z), f32), VM((STEPS, 3, X, Z), f32),
        VM((STEPS, 2, X, Z), f32), VM((STEPS, 1, Z), f32), VM((STEPS, 1, Z), f32),
        VM((3, X, Z), f32), VM((2, X, Z), f32), VM((1, Z), f32), VM((1, Z), f32),
        VM((2, X, Z), f32), VM((2, Y, Z), f32), VM((2, X, Z), f32),
        VM((STEPS, rows, Z), f32), VM((STEPS, rows, Z), f32), VM((NF, Y, 128), f32),
        VM((N, NF, 128), f32), VM((N, NF, 128), f32), VM((NF, gx_n, 128), f32),
        VM((8, 128), f32), VM((N, 8, 128), f32), VM((BMAX, 512), f32),
        dma((9,)), dma((5,)), dma((STEPS, 6)), dma((STEPS, 6)), dma((2,)), dma((2,)),
        dma((gy_n,)), dma((gy_n,)), dma((2,)), dma((2,)),
    ]
    return pl.pallas_call(
        functools.partial(kernel_body, (gx_n, gy_n, X, Y, Z, NB)),
        out_shape=(field, field, field, field, jax.ShapeDtypeStruct((BMAX, 16 * DB), f32)),
        in_specs=[smem] * 6 + [any_spec] * 9,
        out_specs=(any_spec,) * 5,
        scratch_shapes=scratch,
        compiler_params=pltpu.CompilerParams(
            collective_id=0, has_side_effects=True, vmem_limit_bytes=40 * 1024 * 1024
        ),
        name="yee",
    )(mask, owner, ieps, dec, drv, res, e, h, jc, pz, mat, line, slots.reshape(1, -1),
      jnp.asarray(vt), jnp.asarray(wt))


def solution(mesh):
    field = P(None, "gx", "gy", None)
    in_specs = (
        field, field, field, field, P("gx", "gy", None), P(), P(), P(), P(),
        P(None, "gy"), P(), P("gx", "gy", None), P(),
    )
    out_specs = (field, field, field, field, P(("gx", "gy"), None))
    body = functools.partial(shards, gx_n=mesh.shape["gx"], gy_n=mesh.shape["gy"])
    return jax.shard_map(body, mesh=mesh, in_specs=in_specs, out_specs=out_specs, check_vma=False)
```

time: 200 us -> 63.2 us (0.32)
  Pallas kernels: 0 us -> 49.8 us
  matrix products: 41.7 us -> 0 us
  starting transfers between devices: 40.4 us -> 0 us
  local copies, waits for them, and re-layouts: 45.4 us -> 12.3 us
  other arithmetic: 23.5 us -> 0 us
  waiting for transfers between devices: 23.5 us -> 0 us
  blocking collectives: 22.2 us -> 0 us
    pallas_call x0 -> x1, Pallas kernels: none -> 49.8 us  [shards(): pl.pallas_call(functools.partial(kernel_body, (gx_n, gy_n, X, Y, Z, NB)),...]
    dot_general x33 -> x0, matrix products: 41.7 us -> none  [the longest x8 10.4 us: radiate(): jnp.dot(real_rows, sine_part.T, precision=HIGHEST)]
    ppermute x16 -> x0, starting transfers between devices: 40.4 us -> none  [the longest x8 29.9 us: extended(): before = lax.ppermute(last, axis, up)]
    gather x17 -> x0, local copies, waits for them, and re-layouts: 31.1 us -> none  [the longest x8 16.2 us: shards(): inject_e = e_line[inject_index] * region_mask]
    ppermute x16 -> x0, waiting for transfers between devices: 23.5 us -> none  [the longest x8 21.8 us: extended(): after = lax.ppermute(leading, axis, down)]
    all_to_all x1 -> x0, blocking collectives: 17.1 us -> none  [shards(): lax.all_to_all(placed, ('gx', 'gy'), split_axis=0, concat_axis=0, tiled=T...]
    unnamed x31 -> x34, local copies, waits for them, and re-layouts: 2.4 us -> 12.3 us
    all_gather x1 -> x0, blocking collectives: 5.07 us -> none  [shards(): whole_line = lax.all_gather(incident_line, 'gy', axis=1, tiled=True)]
  transfers between devices with their start and end apart: 16 -> 0, of which waited for: 9 -> 0; matrix products, arithmetic and copies ran while one was open for 20% -> 0% of each run, Pallas kernels for 0% -> 0%
where the time goes in v1:
time: 63.2 us; the launch traced here: 62.8 us
  Pallas kernels  49.8 us (79%)
  local copies, waits for them, and re-layouts  12.3 us (19%)
  between operations  0.74 us (1%)
    pallas_call x1, Pallas kernels, shards(): pl.pallas_call(functools.partial(kernel_body, (gx_n, gy_n, X, Y, Z, NB)),...  49.8 us
    unnamed x34, local copies, waits for them, and re-layouts  12.3 us

profile of v1, /device:TPU:0, one launch (start us, length us, event | category | flops | bytes accessed | tf_op | source)
XLA Modules:
  0.0 62.8 jit_solution(9368182551972974636)
XLA Ops:
  0.6 0.0 copy-start.7
  0.6 0.0 copy-start.8
  0.7 0.0 copy-start.9
  0.7 0.0 copy-start.10
  0.7 0.0 copy-start.11
  0.7 0.0 copy-start.12
  0.7 0.0 copy-start.13
  0.7 0.8 %copy.20.mask_s = s32[8,4]{1,0:T(8,128)S(1)} copy(s32[8,4]{0,1:T(4,128)} %param.25) | data formatting | bytes 256 | tf_op args[10]
  1.5 0.0 copy-done.7
  1.5 0.0 copy-done.8
  1.5 0.0 copy-done.9
  1.5 0.0 copy-done.10
  1.5 0.0 copy-done.11
  1.5 0.0 copy-done.12
  1.5 0.0 copy-done.13
  1.5 0.0 copy-start
  1.6 1.1 %copy-done = f32[3,16,32,128]{3,2,1,0:T(8,128)S(1)} copy-done((f32[3,16,32,128]{3,2,1,0:T(8,128)S(1)}, f32[3,16,32,128]{3,2,1,0:T(8,128)}, u32[]{:S(2)}) %copy-start) | copy-done | bytes 786456
  2.7 0.0 copy-start.1
  2.7 1.1 %copy-done.1 = f32[3,16,32,128]{3,2,1,0:T(8,128)S(1)} copy-done((f32[3,16,32,128]{3,2,1,0:T(8,128)S(1)}, f32[3,16,32,128]{3,2,1,0:T(8,128)}, u32[]{:S(2)}) %copy-start.1) | copy-done | bytes 786456
  3.8 0.0 copy-start.2
  3.8 1.1 %copy-done.2 = f32[3,16,32,128]{3,2,1,0:T(8,128)S(1)} copy-done((f32[3,16,32,128]{3,2,1,0:T(8,128)S(1)}, f32[3,16,32,128]{3,2,1,0:T(8,128)}, u32[]{:S(2)}) %copy-start.2) | copy-done | bytes 786456
  4.9 0.0 copy-start.3
  5.0 1.1 %copy-done.3 = f32[3,16,32,128]{3,2,1,0:T(8,128)S(1)} copy-done((f32[3,16,32,128]{3,2,1,0:T(8,128)S(1)}, f32[3,16,32,128]{3,2,1,0:T(8,128)}, u32[]{:S(2)}) %copy-start.3) | copy-done | bytes 786456
  6.1 0.0 copy-start.4
  6.1 0.9 %copy-done.4 = s32[16,32,128]{2,1,0:T(8,128)S(1)} copy-done((s32[16,32,128]{2,1,0:T(8,128)S(1)}, s32[16,32,128]{2,1,0:T(8,128)}, u32[]{:S(2)}) %copy-start.4) | copy-done | bytes 262168
  7.0 0.0 copy-start.5
  7.0 0.9 %copy-done.5 = f32[4,2,64,32]{3,2,1,0:T(8,128)S(1)} copy-done((f32[4,2,64,32]{3,2,1,0:T(8,128)S(1)}, f32[4,2,64,32]{3,2,1,0:T(8,128)}, u32[]{:S(2)}) %copy-start.5) | copy-done | bytes 65560
  8.0 0.0 copy-start.6
  8.0 0.9 %copy-done.6 = f32[2,128,128]{2,1,0:T(8,128)S(1)} copy-done((f32[2,128,128]{2,1,0:T(8,128)S(1)}, f32[2,128,128]{2,1,0:T(8,128)}, u32[]{:S(2)}) %copy-start.6) | copy-done | bytes 131096
  8.9 49.8 %yee.1 = (f32[3,16,32,128]{3,2,1,0:T(8,128)S(1)}, f32[3,16,32,128]{3,2,1,0:T(8,128)S(1)}, f32[3,16,32,128]{3,2,1,0:T(8,128)S(1)}, f32[3,16,32,128]{3,2,1,0:T(8,128)S(1)}, f32[4,512]{1,0:T(4,128)S(1)}) custom-call(s32[8,4]{1,0:T(8,128)S(1)} %copy.20.mask_s, s32[64]{0:T(128)S(1)} %copy-done.8, f32[8]{0:T(128)S(1)} %copy-done.9, f32[8]{0:T(128)S(1)} %copy-done.10, ...), custom_call_target="tpu_custom_call" | custom-call | tf_op jit(solution)/shard_map/yee/pallas_call | solution.py:487
  58.7 0.9 %copy.26 = f32[3,16,32,128]{3,2,1,0:T(8,128)} copy(f32[3,16,32,128]{3,2,1,0:T(8,128)S(1)} %get-tuple-element.10) | data formatting | bytes 1572864
  59.5 0.9 %copy.27 = f32[3,16,32,128]{3,2,1,0:T(8,128)} copy(f32[3,16,32,128]{3,2,1,0:T(8,128)S(1)} %get-tuple-element.11) | data formatting | bytes 1572864
  60.4 0.9 %copy.28 = f32[3,16,32,128]{3,2,1,0:T(8,128)} copy(f32[3,16,32,128]{3,2,1,0:T(8,128)S(1)} %get-tuple-element.12) | data formatting | bytes 1572864
  61.3 0.9 %copy.29 = f32[3,16,32,128]{3,2,1,0:T(8,128)} copy(f32[3,16,32,128]{3,2,1,0:T(8,128)S(1)} %get-tuple-element.13) | data formatting | bytes 1572864
  62.2 0.6 copy.30
Async XLA Ops:
  0.6 0.9 %copy-start.7 = (f32[2,128]{1,0:T(2,128)S(1)}, f32[2,128]{1,0:T(2,128)}, u32[]{:S(2)}) copy-start(f32[2,128]{1,0:T(2,128)} %line_in.1) | copy-start | bytes 3076
  0.6 0.9 %copy-start.8 = (s32[64]{0:T(128)S(1)}, s32[64]{0:T(128)}, u32[]{:S(2)}) copy-start(s32[64]{0:T(128)} %owner_s.1) | copy-start | bytes 772
  0.7 0.9 %copy-start.9 = (f32[8]{0:T(128)S(1)}, f32[8]{0:T(128)}, u32[]{:S(2)}) copy-start(f32[8]{0:T(128)} %ieps_s.1) | copy-start | bytes 100
  0.7 0.8 %copy-start.10 = (f32[8]{0:T(128)S(1)}, f32[8]{0:T(128)}, u32[]{:S(2)}) copy-start(f32[8]{0:T(128)} %dec_s.1) | copy-start | bytes 100
  0.7 0.8 %copy-start.11 = (f32[8]{0:T(128)S(1)}, f32[8]{0:T(128)}, u32[]{:S(2)}) copy-start(f32[8]{0:T(128)} %drv_s.1) | copy-start | bytes 100
  0.7 0.8 %copy-start.12 = (f32[8]{0:T(128)S(1)}, f32[8]{0:T(128)}, u32[]{:S(2)}) copy-start(f32[8]{0:T(128)} %res_s.1) | copy-start | bytes 100
  0.7 0.8 %copy-start.13 = (s32[1,1,128]{2,1,0:T(1,128)S(1)}, s32[1,1,128]{2,1,0:T(1,128)}, u32[]{:S(2)}) copy-start(s32[1,1,128]{2,1,0:T(1,128)} %param.26) | copy-start | bytes 1540
  1.5 1.1 %copy-start = (f32[3,16,32,128]{3,2,1,0:T(8,128)S(1)}, f32[3,16,32,128]{3,2,1,0:T(8,128)}, u32[]{:S(2)}) copy-start(f32[3,16,32,128]{3,2,1,0:T(8,128)} %e_in.1) | copy-start | bytes 2359300
  2.7 1.1 %copy-start.1 = (f32[3,16,32,128]{3,2,1,0:T(8,128)S(1)}, f32[3,16,32,128]{3,2,1,0:T(8,128)}, u32[]{:S(2)}) copy-start(f32[3,16,32,128]{3,2,1,0:T(8,128)} %h_in.1) | copy-start | bytes 2359300
  3.8 1.1 %copy-start.2 = (f32[3,16,32,128]{3,2,1,0:T(8,128)S(1)}, f32[3,16,32,128]{3,2,1,0:T(8,128)}, u32[]{:S(2)}) copy-start(f32[3,16,32,128]{3,2,1,0:T(8,128)} %j_in.1) | copy-start | bytes 2359300
  4.9 1.1 %copy-start.3 = (f32[3,16,32,128]{3,2,1,0:T(8,128)S(1)}, f32[3,16,32,128]{3,2,1,0:T(8,128)}, u32[]{:S(2)}) copy-start(f32[3,16,32,128]{3,2,1,0:T(8,128)} %p_in.1) | copy-start | bytes 2359300
  6.1 0.9 %copy-start.4 = (s32[16,32,128]{2,1,0:T(8,128)S(1)}, s32[16,32,128]{2,1,0:T(8,128)}, u32[]{:S(2)}) copy-start(s32[16,32,128]{2,1,0:T(8,128)} %mat_in.1) | copy-start | bytes 786436
  7.0 0.9 %copy-start.5 = (f32[4,2,64,32]{3,2,1,0:T(8,128)S(1)}, f32[4,2,64,32]{3,2,1,0:T(8,128)}, u32[]{:S(2)}) copy-start(f32[4,2,64,32]{3,2,1,0:T(8,128)} %constant.4.clone.vt_in) | copy-start | bytes 196612
  8.0 0.9 %copy-start.6 = (f32[2,128,128]{2,1,0:T(8,128)S(1)}, f32[2,128,128]{2,1,0:T(8,128)}, u32[]{:S(2)}) copy-start(f32[2,128,128]{2,1,0:T(8,128)} %constant.5.clone.wt_in) | copy-start | bytes 393220

commit v2 on v1

--- a/solution.py
+++ b/solution.py
@@ -62,7 +62,7 @@
     j_out,
     p_out,
     far_out,
-    e, h, j, p, mat, coef, line_b, line_o, slots, vt, wt,
+    e_a, h_a, j_a, p_a, e_b, h_b, j_b, p_b, mat, coef, line_b, line_o, slots, vt, wt,
     xm, xp, ym, yp, ca, cb, ys1, ys0, cas, cbs, hys, gxh, gyh,
     col_e, col_h, ssum, tsend, trecv, tsr, msend, mall, far,
     in_sem, out_sem, snd, rcv, gsnd, grcv, lsnd, lrcv, fsnd, frcv,
@@ -74,6 +74,8 @@
     gx = lax.axis_index("gx")
     gy = lax.axis_index("gy")
     me = gx * GY + gy
+    e, h, j, p = e_a, h_a, j_a, p_a
+    states = ((e_a, h_a, j_a, p_a), (e_b, h_b, j_b, p_b))
 
     loads = [
         pltpu.make_async_copy(e_in, e.at[:, pl.ds(0, X)], in_sem.at[0]),
@@ -158,8 +160,8 @@
             return remote(src, dst, snd.at[n, k], rcv.at[n, k], dx, dy)
 
         return [
-            (has_xp, has_xm, cp(e.at[:, X - 1], xm.at[n], 0, 1, 0)),
-            (has_xm, has_xp, cp(e.at[pl.ds(1, 2), 0], xp.at[n], 1, -1, 0)),
+            (has_xp, has_xm, cp(states[n % 2][0].at[:, X - 1], xm.at[n], 0, 1, 0)),
+            (has_xm, has_xp, cp(states[n % 2][0].at[pl.ds(1, 2), 0], xp.at[n], 1, -1, 0)),
             (has_yp, has_ym, cp(ys1, ym.at[n], 2, 0, 1)),
             (has_ym, has_yp, cp(ys0, yp.at[n], 3, 0, -1)),
             (has_xp & has_ym, has_xm & has_yp, cp(cas, ca.at[n], 4, 1, -1)),
@@ -217,30 +219,6 @@
         return carry
 
     lax.fori_loop(0, X, table, 0)
-
-    loads[6].wait()
-    sl = slots[...]
-    sl_pos = jnp.maximum(sl, 0)
-    sl_x = sl_pos // Y
-    sl_y = sl_pos - sl_x * Y
-    L = sl.shape[-1]
-    one_y = ((lax.broadcasted_iota(jnp.int32, (Y, L), 0) == sl_y) & (sl >= 0)).astype(jnp.bfloat16)
-    one_x = (lax.rem(lax.broadcasted_iota(jnp.int32, (128, L), 0), X) == sl_x).astype(jnp.bfloat16)
-    cell_mask = lax.dot_general(
-        one_y, one_x, (((1,), (1,)), ((), ())), preferred_element_type=jnp.float32
-    )
-
-    def mine(b, carry):
-        cnt, b0, b1, b2, b3 = carry
-        hit = owner_s[b] == me
-        b0 = jnp.where(hit & (cnt == 0), b, b0)
-        b1 = jnp.where(hit & (cnt == 1), b, b1)
-        b2 = jnp.where(hit & (cnt == 2), b, b2)
-        b3 = jnp.where(hit & (cnt == 3), b, b3)
-        return cnt + hit.astype(jnp.int32), b0, b1, b2, b3
-
-    neg = jnp.int32(-1)
-    picks = lax.fori_loop(0, NB, mine, (jnp.int32(0), neg, neg, neg, neg))[1:]
 
     loads[4].wait()
     loads[5].wait()
@@ -289,6 +267,8 @@
 
     finish(first_h)
     for n in range(STEPS):
+        e, h, j, p = states[n % 2]
+        e_n, h_n, j_n, p_n = states[(n + 1) % 2]
         finish(halo0 if n == 0 else pending)
         e[1, X] = xp[n, 0]
         e[2, X] = xp[n, 1]
@@ -305,7 +285,7 @@
         gyh[0] = (gyh[0] - c * ((ys0[1] - ez_m) - fz(ey_m, lane_x))) * keep_y
         gyh[1] = (gyh[1] - c * ((ey_next - ey_m) - (ys0[0] - ex_m))) * keep_y
 
-        def step(x, carry, n=n):
+        def step(x, carry, n=n, e=e, h=h, j=j, p=p, e_n=e_n, h_n=h_n, j_n=j_n, p_n=p_n):
             hy_m, hz_m, plane = carry
             r = pl.ds(x, 1)
             ex, ey, ez = e[0, x], e[1, x], e[2, x]
@@ -314,9 +294,9 @@
             inj_e = jnp.where(lane == z_h, (c * m_own) * col_e[n, pl.ds(x + PAD, Y), :], 0.0)
             hy = h[1, x] - c * (fz(ex, lane) - (ez_x - ez)) + inj_e
             hz = h[2, x] - c * ((ey_x - ey) - (up_y(ex, yp[n, 0, r, :]) - ex))
-            h[0, x] = hx
-            h[1, x] = hy
-            h[2, x] = hz
+            h_n[0, x] = hx
+            h_n[1, x] = hy
+            h_n[2, x] = hz
             inj_h = jnp.where(lane == z_e, m_own * col_h[n, pl.ds(x + PAD, Y), :], 0.0)
             cx = (hz - down_y(hz, gyh[1, r, :])) - bz(hy) + inj_h
             cy = bz(hx) - (hz - hz_m)
@@ -328,9 +308,9 @@
                 po = p[k, x]
                 en = old + ie * (c * curl - jo)
                 jn = dc * jo + dr * en - rs * po
-                e[k, x] = en
-                j[k, x] = jn
-                p[k, x] = po + jn
+                e_n[k, x] = en
+                j_n[k, x] = jn
+                p_n[k, x] = po + jn
                 new.append(en)
             if n < STEPS - 1:
                 for k in range(3):
@@ -343,18 +323,43 @@
             return hy, hz, plane
 
         zero = jnp.zeros((Y, Z), jnp.float32)
-        plane = lax.fori_loop(0, X, step, (gh_y, gh_z, zero))[2]
+        plane = lax.fori_loop(0, X, step, (gh_y, gh_z, zero), unroll=4)[2]
         if n < STEPS - 1:
-            cas[...] = e[0, X - 1, pl.ds(0, 1), :]
-            cbs[...] = e[1, 0, pl.ds(Y - 1, 1), :]
+            cas[...] = e_n[0, X - 1, pl.ds(0, 1), :]
+            cbs[...] = e_n[1, 0, pl.ds(Y - 1, 1), :]
             pending = halo(n + 1)
             start(pending)
+        if n == 0:
+            loads[6].wait()
+            sl = slots[...]
+            sl_pos = jnp.maximum(sl, 0)
+            sl_x = sl_pos // Y
+            sl_y = sl_pos - sl_x * Y
+            L = sl.shape[-1]
+            one_y = ((lax.broadcasted_iota(jnp.int32, (Y, L), 0) == sl_y) & (sl >= 0)).astype(jnp.bfloat16)
+            one_x = (lax.rem(lax.broadcasted_iota(jnp.int32, (128, L), 0), X) == sl_x).astype(jnp.bfloat16)
+            cell_mask = lax.dot_general(
+                one_y, one_x, (((1,), (1,)), ((), ())), preferred_element_type=jnp.float32
+            )
+        if n == 1:
+            def mine(b, carry):
+                cnt, b0, b1, b2, b3 = carry
+                hit = owner_s[b] == me
+                b0 = jnp.where(hit & (cnt == 0), b, b0)
+                b1 = jnp.where(hit & (cnt == 1), b, b1)
+                b2 = jnp.where(hit & (cnt == 2), b, b2)
+                b3 = jnp.where(hit & (cnt == 3), b, b3)
+                return cnt + hit.astype(jnp.int32), b0, b1, b2, b3
+
+            neg = jnp.int32(-1)
+            picks = lax.fori_loop(0, NB, mine, (jnp.int32(0), neg, neg, neg, neg))[1:]
         for f in range(NF):
             wc = math.cos(FREQS[f] * (n + 1))
             ws = -math.sin(FREQS[f] * (n + 1))
             add = jnp.where(lane < 4 * X, wc, ws) * plane
             ssum[f] = add if n == 0 else ssum[f] + add
 
+    e, h, j, p = states[STEPS % 2]
     stores = [
         pltpu.make_async_copy(e.at[:, pl.ds(0, X)], e_out, out_sem.at[0]),
         pltpu.make_async_copy(h, h_out, out_sem.at[1]),
@@ -464,6 +469,7 @@
     vt, wt = phase_tables(gx_n, gy_n, X, Y, NB * DB)
     f32 = jnp.float32
     any_spec = pl.BlockSpec(memory_space=pl.ANY)
+    hbm = pl.BlockSpec(memory_space=pltpu.HBM)
     smem = pl.BlockSpec(memory_space=pltpu.SMEM)
     field = jax.ShapeDtypeStruct((3, X, Y, Z), f32)
     rows = X + Y + 2 * PAD
@@ -471,7 +477,8 @@
     dma = pltpu.SemaphoreType.DMA
     scratch = [
         VM((3, X + 1, Y, Z), f32), VM((3, X, Y, Z), f32), VM((3, X, Y, Z), f32),
-        VM((3, X, Y, Z), f32), VM((X, Y, Z), jnp.int32), VM((4, X, Y, Z), f32),
+        VM((3, X, Y, Z), f32), VM((3, X + 1, Y, Z), f32), VM((3, X, Y, Z), f32),
+        VM((3, X, Y, Z), f32), VM((3, X, Y, Z), f32), VM((X, Y, Z), jnp.int32), VM((4, X, Y, Z), f32),
         VM((gy_n,) + line.shape, f32), VM(line.shape, f32), VM((1, slots.shape[-1]), jnp.int32),
         VM(vt.shape[1:], f32), VM(wt.shape, f32),
         VM((STEPS, 3, Y, Z), f32), VM((STEPS, 2, Y, Z), f32), VM((STEPS, 3, X, Z), f32),
@@ -484,18 +491,19 @@
         dma((9,)), dma((5,)), dma((STEPS, 6)), dma((STEPS, 6)), dma((2,)), dma((2,)),
         dma((gy_n,)), dma((gy_n,)), dma((2,)), dma((2,)),
     ]
-    return pl.pallas_call(
+    outs = pl.pallas_call(
         functools.partial(kernel_body, (gx_n, gy_n, X, Y, Z, NB)),
         out_shape=(field, field, field, field, jax.ShapeDtypeStruct((BMAX, 16 * DB), f32)),
-        in_specs=[smem] * 6 + [any_spec] * 9,
+        in_specs=[smem] * 6 + [hbm] * 9,
         out_specs=(any_spec,) * 5,
         scratch_shapes=scratch,
         compiler_params=pltpu.CompilerParams(
-            collective_id=0, has_side_effects=True, vmem_limit_bytes=40 * 1024 * 1024
+            collective_id=0, has_side_effects=True, vmem_limit_bytes=60 * 1024 * 1024
         ),
         name="yee",
     )(mask, owner, ieps, dec, drv, res, e, h, jc, pz, mat, line, slots.reshape(1, -1),
       jnp.asarray(vt), jnp.asarray(wt))
+    return outs
 
 
 def solution(mesh):

time: 63.2 us -> 48.3 us (0.76)
  Pallas kernels: 49.8 us -> 39.5 us
  local copies, waits for them, and re-layouts: 12.3 us -> 7.8 us
    pallas_call x1, Pallas kernels: 49.8 us -> 39.5 us  [shards(): pl.pallas_call(functools.partial(kernel_body, (gx_n, gy_n, X, Y, Z, NB)),...]
    unnamed x34 -> x14, local copies, waits for them, and re-layouts: 12.3 us -> 7.8 us
where the time goes in v2:
time: 48.3 us; the launch traced here: 48 us
  Pallas kernels  39.5 us (82%)
  local copies, waits for them, and re-layouts  7.8 us (16%)
  between operations  0.65 us (1%)
    pallas_call x1, Pallas kernels, shards(): pl.pallas_call(functools.partial(kernel_body, (gx_n, gy_n, X, Y, Z, NB)),...  39.5 us
    unnamed x14, local copies, waits for them, and re-layouts  7.8 us

profile of v2, /device:TPU:0, one launch (start us, length us, event | category | flops | bytes accessed | tf_op | source)
XLA Modules:
  0.0 48.0 jit_solution(18201547860454329902)
XLA Ops:
  0.6 1.3 %copy.20.mask_s = s32[8,4]{1,0:T(8,128)} copy(s32[8,4]{0,1:T(4,128)} %param.25) | data formatting | bytes 256 | tf_op args[10]
  2.0 39.5 %yee.1 = (f32[3,16,32,128]{3,2,1,0:T(8,128)}, f32[3,16,32,128]{3,2,1,0:T(8,128)}, f32[3,16,32,128]{3,2,1,0:T(8,128)}, f32[3,16,32,128]{3,2,1,0:T(8,128)}, f32[4,512]{1,0:T(4,128)}) custom-call(s32[8,4]{1,0:T(8,128)} %copy.20.mask_s, s32[64]{0:T(128)} %owner_s.1, f32[8]{0:T(128)} %ieps_s.1, f32[8]{0:T(128)} %dec_s.1, f32[8]{0:T(128)} %drv_s.1, f32[8]{0:T(128)} %res_s.1, ...), custom_call_target="tpu_custom_call" | custom-call | tf_op jit(solution)/shard_map/yee/pallas_call | solution.py:494
  41.5 0.0 copy-start.2
  41.5 2.1 %copy.26 = f32[3,16,32,128]{3,2,1,0:T(8,128)} copy(f32[3,16,32,128]{3,2,1,0:T(8,128)} %get-tuple-element.10) | data formatting | bytes 1572864
  43.7 0.0 copy-done.2
  43.7 0.0 copy-start.1
  43.7 0.9 %copy.27 = f32[3,16,32,128]{3,2,1,0:T(8,128)} copy(f32[3,16,32,128]{3,2,1,0:T(8,128)S(1)} %copy-done.2) | data formatting | bytes 1572864
  44.6 0.5 %copy-done.1 = f32[3,16,32,128]{3,2,1,0:T(8,128)S(1)} copy-done((f32[3,16,32,128]{3,2,1,0:T(8,128)S(1)}, f32[3,16,32,128]{3,2,1,0:T(8,128)}, u32[]{:S(2)}) %copy-start.1) | copy-done | bytes 786456
  45.1 0.0 copy-start
  45.1 0.9 %copy.28 = f32[3,16,32,128]{3,2,1,0:T(8,128)} copy(f32[3,16,32,128]{3,2,1,0:T(8,128)S(1)} %copy-done.1) | data formatting | bytes 1572864
  46.0 0.5 %copy-done = f32[3,16,32,128]{3,2,1,0:T(8,128)S(1)} copy-done((f32[3,16,32,128]{3,2,1,0:T(8,128)S(1)}, f32[3,16,32,128]{3,2,1,0:T(8,128)}, u32[]{:S(2)}) %copy-start) | copy-done | bytes 786456
  46.5 0.0 copy-start.3
  46.5 0.9 %copy.29 = f32[3,16,32,128]{3,2,1,0:T(8,128)} copy(f32[3,16,32,128]{3,2,1,0:T(8,128)S(1)} %copy-done) | data formatting | bytes 1572864
  47.4 0.0 copy-done.3
  47.4 0.6 %copy.30 = f32[4,512]{1,0:T(4,128)} copy(f32[4,512]{1,0:T(4,128)S(1)} %copy-done.3) | data formatting | bytes 16384
Async XLA Ops:
  41.5 2.1 %copy-start.2 = (f32[3,16,32,128]{3,2,1,0:T(8,128)S(1)}, f32[3,16,32,128]{3,2,1,0:T(8,128)}, u32[]{:S(2)}) copy-start(f32[3,16,32,128]{3,2,1,0:T(8,128)} %get-tuple-element.11) | copy-start | bytes 2359300
  43.7 1.4 %copy-start.1 = (f32[3,16,32,128]{3,2,1,0:T(8,128)S(1)}, f32[3,16,32,128]{3,2,1,0:T(8,128)}, u32[]{:S(2)}) copy-start(f32[3,16,32,128]{3,2,1,0:T(8,128)} %get-tuple-element.12) | copy-start | bytes 2359300
  45.1 1.4 %copy-start = (f32[3,16,32,128]{3,2,1,0:T(8,128)S(1)}, f32[3,16,32,128]{3,2,1,0:T(8,128)}, u32[]{:S(2)}) copy-start(f32[3,16,32,128]{3,2,1,0:T(8,128)} %get-tuple-element.13) | copy-start | bytes 2359300
  46.5 0.9 %copy-start.3 = (f32[4,512]{1,0:T(4,128)S(1)}, f32[4,512]{1,0:T(4,128)}, u32[]{:S(2)}) copy-start(f32[4,512]{1,0:T(4,128)} %get-tuple-element.14) | copy-start | bytes 24580

commit v3 on v2

--- a/solution.py
+++ b/solution.py
@@ -65,7 +65,7 @@
     e_a, h_a, j_a, p_a, e_b, h_b, j_b, p_b, mat, coef, line_b, line_o, slots, vt, wt,
     xm, xp, ym, yp, ca, cb, ys1, ys0, cas, cbs, hys, gxh, gyh,
     col_e, col_h, ssum, tsend, trecv, tsr, msend, mall, far,
-    in_sem, out_sem, snd, rcv, gsnd, grcv, lsnd, lrcv, fsnd, frcv,
+    eh_sem, in_sem, out_sem, snd, rcv, gsnd, grcv, lsnd, lrcv, fsnd, frcv,
 ):
     GX, GY, X, Y, Z, NB = dims
     N = GX * GY
@@ -78,8 +78,8 @@
     states = ((e_a, h_a, j_a, p_a), (e_b, h_b, j_b, p_b))
 
     loads = [
-        pltpu.make_async_copy(e_in, e.at[:, pl.ds(0, X)], in_sem.at[0]),
-        pltpu.make_async_copy(h_in, h, in_sem.at[1]),
+        [pltpu.make_async_copy(e_in.at[k], e.at[k, pl.ds(0, X)], eh_sem.at[k]) for k in range(3)],
+        [pltpu.make_async_copy(h_in.at[k], h.at[k], eh_sem.at[3 + k]) for k in range(3)],
         pltpu.make_async_copy(line_in, line_o, in_sem.at[2]),
         pltpu.make_async_copy(mat_in, mat, in_sem.at[3]),
         pltpu.make_async_copy(j_in, j, in_sem.at[4]),
@@ -88,7 +88,7 @@
         pltpu.make_async_copy(vt_in.at[gy], vt, in_sem.at[7]),
         pltpu.make_async_copy(wt_in, wt, in_sem.at[8]),
     ]
-    for cp in loads:
+    for cp in loads[0] + loads[1] + loads[2:]:
         cp.start()
 
     has_xm, has_xp = gx > 0, gx < GX - 1
@@ -120,6 +120,10 @@
     def _():
         cb[...] = jnp.zeros_like(cb)
 
+    for ref in (e_a, e_b):
+        for k in (1, 2):
+            ref[k, X] = jnp.zeros((Y, Z), jnp.float32)
+
     barrier = pltpu.get_barrier_semaphore()
 
     def greet(i, carry):
@@ -129,8 +133,8 @@
 
     lax.fori_loop(1, N, greet, 0)
 
-    loads[0].wait()
-    loads[1].wait()
+    for cp in loads[0] + loads[1]:
+        cp.wait()
 
     def pack(x, carry):
         r = pl.ds(x, 1)
@@ -248,8 +252,8 @@
         ev = (ev - c * (hv - pltpu.roll(ho, 1, 0))) * keep_v
         od = (od - c * (ho - hv)) * keep_v
 
-    m_own = mask_s[gx, gy].astype(jnp.float32)
-    m_left = mask_s[jnp.maximum(gx - 1, 0), gy].astype(jnp.float32)
+    m_own = mask_s[gy, gx].astype(jnp.float32)
+    m_left = mask_s[gy, jnp.maximum(gx - 1, 0)].astype(jnp.float32)
     keep_x = has_xm.astype(jnp.float32)
     keep_y = has_ym.astype(jnp.float32)
 
@@ -265,13 +269,49 @@
     def down_y(v, edge):
         return jnp.where(row == 0, edge, pltpu.roll(v, 1, 0))
 
+    def magnetic(n):
+        e, h = states[n % 2][:2]
+        h_n = states[(n + 1) % 2][1]
+
+        def body(x, carry):
+            ex, ey, ez = e[0, x], e[1, x], e[2, x]
+            ey_x, ez_x = e[1, x + 1], e[2, x + 1]
+            inj_e = jnp.where(lane == z_h, (c * m_own) * col_e[n, pl.ds(x + PAD, Y), :], 0.0)
+            h_n[0, x] = h[0, x] - c * ((up_y(ez, 0.0) - ez) - fz(ey, lane))
+            h_n[1, x] = h[1, x] - c * (fz(ex, lane) - (ez_x - ez)) + inj_e
+            h_n[2, x] = h[2, x] - c * ((ey_x - ey) - (up_y(ex, 0.0) - ex))
+            return carry
+
+        lax.fori_loop(0, X, body, 0, unroll=4)
+
+    def matter(n):
+        j, p = states[n % 2][2:]
+        e_n, _, j_n, p_n = states[(n + 1) % 2]
+
+        def body(x, carry):
+            dc, dr, rs = coef[1, x], coef[2, x], coef[3, x]
+            for k in range(3):
+                po = p[k, x]
+                jn = dc * j[k, x] + dr * e_n[k, x] - rs * po
+                j_n[k, x] = jn
+                p_n[k, x] = po + jn
+            return carry
+
+        lax.fori_loop(0, X, body, 0, unroll=4)
+
+    magnetic(0)
     finish(first_h)
     for n in range(STEPS):
         e, h, j, p = states[n % 2]
         e_n, h_n, j_n, p_n = states[(n + 1) % 2]
         finish(halo0 if n == 0 else pending)
-        e[1, X] = xp[n, 0]
-        e[2, X] = xp[n, 1]
+        h_n[1, X - 1] = h_n[1, X - 1] + c * xp[n, 1]
+        h_n[2, X - 1] = h_n[2, X - 1] - c * xp[n, 0]
+        edge = pl.ds(Y - 1, 1)
+        for x in range(X):
+            r = pl.ds(x, 1)
+            h_n[0, x, edge, :] = h_n[0, x, edge, :] - c * yp[n, 1, r, :]
+            h_n[2, x, edge, :] = h_n[2, x, edge, :] + c * yp[n, 0, r, :]
         ex_m, ey_m, ez_m = xm[n, 0], xm[n, 1], xm[n, 2]
         inj = jnp.where(lane == z_h, (c * m_left) * col_e[n, pl.ds(PAD - 1, Y), :], 0.0)
         gh_y = gxh[0] - c * (fz(ex_m, lane) - (e[2, 0] - ez_m)) + inj
@@ -285,45 +325,28 @@
         gyh[0] = (gyh[0] - c * ((ys0[1] - ez_m) - fz(ey_m, lane_x))) * keep_y
         gyh[1] = (gyh[1] - c * ((ey_next - ey_m) - (ys0[0] - ex_m))) * keep_y
 
-        def step(x, carry, n=n, e=e, h=h, j=j, p=p, e_n=e_n, h_n=h_n, j_n=j_n, p_n=p_n):
-            hy_m, hz_m, plane = carry
+        def step(x, carry, n=n, e=e, j=j, e_n=e_n, h_n=h_n):
+            hy_m, hz_m = carry
             r = pl.ds(x, 1)
-            ex, ey, ez = e[0, x], e[1, x], e[2, x]
-            ey_x, ez_x = e[1, x + 1], e[2, x + 1]
-            hx = h[0, x] - c * ((up_y(ez, yp[n, 1, r, :]) - ez) - fz(ey, lane))
-            inj_e = jnp.where(lane == z_h, (c * m_own) * col_e[n, pl.ds(x + PAD, Y), :], 0.0)
-            hy = h[1, x] - c * (fz(ex, lane) - (ez_x - ez)) + inj_e
-            hz = h[2, x] - c * ((ey_x - ey) - (up_y(ex, yp[n, 0, r, :]) - ex))
-            h_n[0, x] = hx
-            h_n[1, x] = hy
-            h_n[2, x] = hz
+            hx, hy, hz = h_n[0, x], h_n[1, x], h_n[2, x]
             inj_h = jnp.where(lane == z_e, m_own * col_h[n, pl.ds(x + PAD, Y), :], 0.0)
             cx = (hz - down_y(hz, gyh[1, r, :])) - bz(hy) + inj_h
             cy = bz(hx) - (hz - hz_m)
             cz = (hy - hy_m) - (hx - down_y(hx, gyh[0, r, :]))
-            ie, dc, dr, rs = coef[0, x], coef[1, x], coef[2, x], coef[3, x]
+            ie = coef[0, x]
             new = []
-            for k, (old, curl) in enumerate(((ex, cx), (ey, cy), (ez, cz))):
-                jo = j[k, x]
-                po = p[k, x]
-                en = old + ie * (c * curl - jo)
-                jn = dc * jo + dr * en - rs * po
+            for k, curl in enumerate((cx, cy, cz)):
+                en = e[k, x] + ie * (c * curl - j[k, x])
                 e_n[k, x] = en
-                j_n[k, x] = jn
-                p_n[k, x] = po + jn
                 new.append(en)
             if n < STEPS - 1:
                 for k in range(3):
                     ys1[k, r, :] = new[k][Y - 1 : Y]
                 ys0[0, r, :] = new[0][0:1]
                 ys0[1, r, :] = new[2][0:1]
-            l64 = lax.rem(lane, 4 * X)
-            for k, val in enumerate((new[0], new[1], hx, hy)):
-                plane = jnp.where(l64 == k * X + x, val[:, z_s : z_s + 1], plane)
-            return hy, hz, plane
-
-        zero = jnp.zeros((Y, Z), jnp.float32)
-        plane = lax.fori_loop(0, X, step, (gh_y, gh_z, zero), unroll=4)[2]
+            return hy, hz
+
+        lax.fori_loop(0, X, step, (gh_y, gh_z), unroll=4)
         if n < STEPS - 1:
             cas[...] = e_n[0, X - 1, pl.ds(0, 1), :]
             cbs[...] = e_n[1, 0, pl.ds(Y - 1, 1), :]
@@ -353,12 +376,24 @@
 
             neg = jnp.int32(-1)
             picks = lax.fori_loop(0, NB, mine, (jnp.int32(0), neg, neg, neg, neg))[1:]
+        l64 = lax.rem(lane, 4 * X)
+
+        def surface(x, plane, e_n=e_n, h_n=h_n, l64=l64):
+            for k, ref in enumerate((e_n.at[0], e_n.at[1], h_n.at[0], h_n.at[1])):
+                val = ref[x]
+                plane = jnp.where(l64 == k * X + x, val[:, z_s : z_s + 1], plane)
+            return plane
+
+        plane = lax.fori_loop(0, X, surface, jnp.zeros((Y, Z), jnp.float32), unroll=4)
         for f in range(NF):
             wc = math.cos(FREQS[f] * (n + 1))
             ws = -math.sin(FREQS[f] * (n + 1))
             add = jnp.where(lane < 4 * X, wc, ws) * plane
             ssum[f] = add if n == 0 else ssum[f] + add
 
+        if n < STEPS - 1:
+            matter(n)
+            magnetic(n + 1)
     e, h, j, p = states[STEPS % 2]
     stores = [
         pltpu.make_async_copy(e.at[:, pl.ds(0, X)], e_out, out_sem.at[0]),
@@ -366,8 +401,8 @@
         pltpu.make_async_copy(j, j_out, out_sem.at[2]),
         pltpu.make_async_copy(p, p_out, out_sem.at[3]),
     ]
-    for cp in stores:
-        cp.start()
+    stores[0].start()
+    stores[1].start()
 
     loads[7].wait()
     loads[8].wait()
@@ -388,6 +423,9 @@
         return carry
 
     lax.fori_loop(1, N, send_t, 0)
+    matter(STEPS - 1)
+    stores[2].start()
+    stores[3].start()
     trecv[me] = tsend[me]
     part = pl.ds(0, N - 1)
     pltpu.make_async_copy(trecv.at[part], trecv.at[part], frcv.at[0]).wait()
@@ -462,6 +500,26 @@
     last.wait()
 
 
+def write_body(*refs):
+    bufs, (far_b, s_in, s_out) = refs[10:14], refs[14:]
+    far_load = pltpu.make_async_copy(refs[4], far_b, s_in.at[4, 0])
+    far_store = pltpu.make_async_copy(far_b, refs[9], s_out.at[4, 0])
+    loads, stores = [], []
+    for i in range(4):
+        for k in range(3):
+            loads.append(pltpu.make_async_copy(refs[i].at[k], bufs[i].at[k], s_in.at[i, k]))
+            stores.append(pltpu.make_async_copy(bufs[i].at[k], refs[5 + i].at[k], s_out.at[i, k]))
+    loads.append(far_load)
+    stores.append(far_store)
+    for cp in loads:
+        cp.start()
+    for a, b in zip(loads, stores):
+        a.wait()
+        b.start()
+    for cp in stores:
+        cp.wait()
+
+
 def shards(e, h, jc, pz, mat, ieps, dec, drv, res, line, mask, slots, owner, gx_n=0, gy_n=0):
     _, X, Y, Z = e.shape
     N = gx_n * gy_n
@@ -488,7 +546,7 @@
         VM((STEPS, rows, Z), f32), VM((STEPS, rows, Z), f32), VM((NF, Y, 128), f32),
         VM((N, NF, 128), f32), VM((N, NF, 128), f32), VM((NF, gx_n, 128), f32),
         VM((8, 128), f32), VM((N, 8, 128), f32), VM((BMAX, 512), f32),
-        dma((9,)), dma((5,)), dma((STEPS, 6)), dma((STEPS, 6)), dma((2,)), dma((2,)),
+        dma((6,)), dma((9,)), dma((5,)), dma((STEPS, 6)), dma((STEPS, 6)), dma((2,)), dma((2,)),
         dma((gy_n,)), dma((gy_n,)), dma((2,)), dma((2,)),
     ]
     outs = pl.pallas_call(
@@ -501,9 +559,18 @@
             collective_id=0, has_side_effects=True, vmem_limit_bytes=60 * 1024 * 1024
         ),
         name="yee",
-    )(mask, owner, ieps, dec, drv, res, e, h, jc, pz, mat, line, slots.reshape(1, -1),
+    )(mask.T, owner, ieps, dec, drv, res, e, h, jc, pz, mat, line, slots.reshape(1, -1),
       jnp.asarray(vt), jnp.asarray(wt))
-    return outs
+    bufs = [VM((3, X, Y, Z), f32)] * 4
+    return pl.pallas_call(
+        write_body,
+        out_shape=tuple(jax.ShapeDtypeStruct(o.shape, o.dtype) for o in outs),
+        in_specs=[any_spec] * 5,
+        out_specs=(any_spec,) * 5,
+        scratch_shapes=bufs + [VM((BMAX, 16 * DB), f32), dma((5, 3)), dma((5, 3))],
+        compiler_params=pltpu.CompilerParams(vmem_limit_bytes=60 * 1024 * 1024),
+        name="write",
+    )(*outs)
 
 
 def solution(mesh):

time: 48.3 us -> 40.6 us (0.84)
  local copies, waits for them, and re-layouts: 7.8 us -> 0 us
    unnamed x14 -> x0, local copies, waits for them, and re-layouts: 7.8 us -> none
    pallas_call x0 -> x1, Pallas kernels: none -> 2.87 us  [shards(): pl.pallas_call(write_body, out_shape=tuple((jax.ShapeDtypeStruct(o.shape,...]
    pallas_call x1, Pallas kernels: 39.5 us -> 37 us  [shards(): pl.pallas_call(functools.partial(kernel_body, (gx_n, gy_n, X, Y, Z, NB)),...]
where the time goes in v3:
time: 40.6 us; the launch traced here: 40.5 us
  Pallas kernels  39.8 us (98%)
  between operations  0.65 us (2%)
    pallas_call x1, Pallas kernels, shards(): pl.pallas_call(functools.partial(kernel_body, (gx_n, gy_n, X, Y, Z, NB)),...  37 us
    pallas_call x1, Pallas kernels, shards(): pl.pallas_call(write_body, out_shape=tuple((jax.ShapeDtypeStruct(o.shape,...  2.87 us

profile of v3, /device:TPU:0, one launch (start us, length us, event | category | flops | bytes accessed | tf_op | source)
XLA Modules:
  0.0 40.5 jit_solution(6743291191657915436)
XLA Ops:
  0.6 37.0 %yee.1 = (f32[3,16,32,128]{3,2,1,0:T(8,128)}, f32[3,16,32,128]{3,2,1,0:T(8,128)}, f32[3,16,32,128]{3,2,1,0:T(8,128)}, f32[3,16,32,128]{3,2,1,0:T(8,128)}, f32[4,512]{1,0:T(4,128)}) custom-call(s32[4,8]{1,0:T(4,128)} %bitcast.2, s32[64]{0:T(128)} %owner_s.1, f32[8]{0:T(128)} %ieps_s.1, f32[8]{0:T(128)} %dec_s.1, f32[8]{0:T(128)} %drv_s.1, f32[8]{0:T(128)} %res_s.1, ...), custom_call_target="tpu_custom_call" | custom-call | tf_op jit(solution)/shard_map/yee/pallas_call | solution.py:552
  37.6 2.9 %write.1 = (f32[3,16,32,128]{3,2,1,0:T(8,128)}, f32[3,16,32,128]{3,2,1,0:T(8,128)}, f32[3,16,32,128]{3,2,1,0:T(8,128)}, f32[3,16,32,128]{3,2,1,0:T(8,128)}, f32[4,512]{1,0:T(4,128)}) custom-call(f32[3,16,32,128]{3,2,1,0:T(8,128)} %get-tuple-element.10.refs_0_, f32[3,16,32,128]{3,2,1,0:T(8,128)} %get-tuple-element.11.refs_1_, ...), custom_call_target="tpu_custom_call" | custom-call | tf_op jit(solution)/shard_map/write/pallas_call | solution.py:565

commit v4 on v3

--- a/solution.py
+++ b/solution.py
@@ -88,7 +88,7 @@
         pltpu.make_async_copy(vt_in.at[gy], vt, in_sem.at[7]),
         pltpu.make_async_copy(wt_in, wt, in_sem.at[8]),
     ]
-    for cp in loads[0] + loads[1] + loads[2:]:
+    for cp in loads[0] + loads[1] + loads[2:4]:
         cp.start()
 
     has_xm, has_xp = gx > 0, gx < GX - 1
@@ -135,6 +135,8 @@
 
     for cp in loads[0] + loads[1]:
         cp.wait()
+    for cp in loads[4:]:
+        cp.start()
 
     def pack(x, carry):
         r = pl.ds(x, 1)
@@ -146,7 +148,7 @@
         hys[1, r, :] = h[2, x, pl.ds(Y - 1, 1), :]
         return carry
 
-    lax.fori_loop(0, X, pack, 0)
+    lax.fori_loop(0, X, pack, 0, unroll=4)
     cas[...] = e[0, X - 1, pl.ds(0, 1), :]
     cbs[...] = e[1, 0, pl.ds(Y - 1, 1), :]
     loads[2].wait()
@@ -222,7 +224,7 @@
             coef[k, x] = outs[k]
         return carry
 
-    lax.fori_loop(0, X, table, 0)
+    lax.fori_loop(0, X, table, 0, unroll=2)
 
     loads[4].wait()
     loads[5].wait()
@@ -346,7 +348,7 @@
                 ys0[1, r, :] = new[2][0:1]
             return hy, hz
 
-        lax.fori_loop(0, X, step, (gh_y, gh_z), unroll=4)
+        lax.fori_loop(0, X, step, (gh_y, gh_z), unroll=8)
         if n < STEPS - 1:
             cas[...] = e_n[0, X - 1, pl.ds(0, 1), :]
             cbs[...] = e_n[1, 0, pl.ds(Y - 1, 1), :]

time: 40.6 us -> 40.2 us (level)
    pallas_call x1, Pallas kernels: 37 us -> 36.5 us  [shards(): pl.pallas_call(functools.partial(kernel_body, (gx_n, gy_n, X, Y, Z, NB)),...]
where the time goes in v4:
time: 40.2 us; the launch traced here: 40 us
  Pallas kernels  39.4 us (98%)
  between operations  0.65 us (2%)
    pallas_call x1, Pallas kernels, shards(): pl.pallas_call(functools.partial(kernel_body, (gx_n, gy_n, X, Y, Z, NB)),...  36.5 us
    pallas_call x1, Pallas kernels, shards(): pl.pallas_call(write_body, out_shape=tuple((jax.ShapeDtypeStruct(o.shape,...  2.87 us

profile of v4, /device:TPU:0, one launch (start us, length us, event | category | flops | bytes accessed | tf_op | source)
XLA Modules:
  0.0 40.0 jit_solution(5396075372482164420)
XLA Ops:
  0.6 36.5 %yee.1 = (f32[3,16,32,128]{3,2,1,0:T(8,128)}, f32[3,16,32,128]{3,2,1,0:T(8,128)}, f32[3,16,32,128]{3,2,1,0:T(8,128)}, f32[3,16,32,128]{3,2,1,0:T(8,128)}, f32[4,512]{1,0:T(4,128)}) custom-call(s32[4,8]{1,0:T(4,128)} %bitcast.2, s32[64]{0:T(128)} %owner_s.1, f32[8]{0:T(128)} %ieps_s.1, f32[8]{0:T(128)} %dec_s.1, f32[8]{0:T(128)} %drv_s.1, f32[8]{0:T(128)} %res_s.1, ...), custom_call_target="tpu_custom_call" | custom-call | tf_op jit(solution)/shard_map/yee/pallas_call | solution.py:554
  37.1 2.9 %write.1 = (f32[3,16,32,128]{3,2,1,0:T(8,128)}, f32[3,16,32,128]{3,2,1,0:T(8,128)}, f32[3,16,32,128]{3,2,1,0:T(8,128)}, f32[3,16,32,128]{3,2,1,0:T(8,128)}, f32[4,512]{1,0:T(4,128)}) custom-call(f32[3,16,32,128]{3,2,1,0:T(8,128)} %get-tuple-element.10.refs_0_, f32[3,16,32,128]{3,2,1,0:T(8,128)} %get-tuple-element.11.refs_1_, ...), custom_call_target="tpu_custom_call" | custom-call | tf_op jit(solution)/shard_map/write/pallas_call | solution.py:567
